TPU v7x, 256 devices: a whole 4x4x8 slice. The times are simulated.
256 devices in a mesh: face: 8 (over x_hi, y), slab: 32 (over x_lo, z, core).
Axes of the slice: x: 4 (x_hi: 2, x_lo: 2; x = x_hi * 2 + x_lo), y: 4, z: 8, core: 2. Of those that a mesh axis runs over, the one named last changes fastest.
Arguments:
- activations: bfloat16 [8, 256, 512, 128], P('face', 'slab'), may hold values from -6 to 6
- cotangent: bfloat16 [8, 256, 512, 128], P('face', 'slab'), may hold values from -6 to 6
- conv_weight: float32 [9, 128], replicated, may hold values from -2 to 2
- norm_gain: float32 [128], replicated, may hold values from 0.1 to 1.9
- w_in: bfloat16 [128, 512], replicated, may hold values from -0.5 to 0.5
- w_out: bfloat16 [512, 128], replicated, may hold values from -0.25 to 0.25
- layer_scale: float32 [128], replicated, may hold values from 0.25 to 2
- neighbours: int32 [8, 32, 2, 4], P('face', 'slab'), may hold values from 0 to 31, as said below
Outputs:
- input_gradient: bfloat16 [8, 256, 512, 128], P('face', 'slab')
- conv_grad: float32 [9, 128], replicated
- gain_grad: float32 [128], replicated
- in_grad: float32 [128, 512], replicated
- out_grad: float32 [512, 128], replicated
- scale_grad: float32 [128], replicated
Inputs may be any that keep to these rules, and one draw needn't show every extreme that they name: `neighbours`: entry [f, s, e] = (source face, source slab, source edge, code). Side edges of the 8 faces are joined in pairs, never an edge with itself; both edges of a pair name each other with the same code. For one face and edge all slabs have the same source face, edge and code; the source slab is s for code 0 and 31 - s for code 1.
All inputs are finite; a program needn't handle non-finite values.
Results may differ from a plain program's by a relative error of at most 0.0076.
Values may be sent and summed in bfloat16 or wider, within the bound.
A program may use at most 128 MiB of HBM per device.

v0:
```python
from functools import partial

import jax
import jax.numpy as jnp
from jax import lax
from jax.sharding import PartitionSpec as P

DILATION_STEP = 2


EPSILON = 1e-06


def from_partner(value, axis, stride):
    mask = 2**stride
    pairs = [(source, source ^ mask) for source in range(lax.axis_size(axis))]
    return lax.ppermute(value, axis, pairs)


def padded(cells, sides, width):
    for axis, dim in sides:
        count = lax.axis_size(axis)
        ends = count - 1
        head = lax.slice_in_dim(cells, 0, width, axis=dim)
        tail = lax.slice_in_dim(cells, cells.shape[dim] - width, cells.shape[dim], axis=dim)
        cells = jnp.concatenate(
            [
                lax.ppermute(tail, axis, [(i, (i + 1) % count) for i in range(ends)]),
                cells,
                lax.ppermute(head, axis, [((i + 1) % count, i) for i in range(ends)]),
            ],
            axis=dim,
        )
    return cells


def from_behind(value, axis, steps):
    count = lax.axis_size(axis)
    leading, last = (max(0, -steps), min(count, count - steps))
    return lax.ppermute(value, axis, [(source, source + steps) for source in range(leading, last)])


def dilated(weights, padded_input):
    row_total = padded_input.shape[0] - 2 * DILATION_STEP
    column_total = padded_input.shape[1] - 2 * DILATION_STEP
    accumulated = jnp.zeros((row_total, column_total, padded_input.shape[2]), jnp.float32)
    for row_offset in range(3):
        for column_offset in range(3):
            sliding_view = padded_input[
                row_offset * DILATION_STEP : row_offset * DILATION_STEP + row_total,
                column_offset * DILATION_STEP : column_offset * DILATION_STEP + column_total,
            ]
            accumulated = accumulated + weights[3 * row_offset + column_offset] * sliding_view
    return accumulated


def transposed(weights, source, out_rows, out_cols):
    accumulated = jnp.zeros((out_rows, out_cols, source.shape[2]), jnp.float32)
    for row_offset in range(3):
        for column_offset in range(3):
            row_begin = 2 * DILATION_STEP - row_offset * DILATION_STEP
            column_begin = 2 * DILATION_STEP - column_offset * DILATION_STEP
            sliding_view = source[
                row_begin : row_begin + out_rows, column_begin : column_begin + out_cols
            ]
            accumulated = accumulated + weights[3 * row_offset + column_offset] * sliding_view
    return accumulated


def norm_backward(upstream, normed, inverse):
    return inverse * (
        upstream
        - jnp.mean(upstream, -1, keepdims=True)
        - normed * jnp.mean(upstream * normed, -1, keepdims=True)
    )


def mlp_pass(conv_out, upstream, norm_gain, w_in, w_out, layer_scale):
    channels = conv_out.shape[-1]
    features = conv_out.reshape(-1, channels)
    average = jnp.mean(features, -1, keepdims=True)
    centred = features - average
    variance = jnp.mean(centred * centred, -1, keepdims=True)
    inverse = lax.rsqrt(variance + EPSILON)
    normed = centred * inverse
    scaled = (normed * norm_gain).astype(jnp.bfloat16)
    hidden = jnp.dot(scaled, w_in, preferred_element_type=jnp.float32)
    activated, gelu_back = jax.vjp(partial(jax.nn.gelu, approximate=False), hidden)
    activated_b = activated.astype(jnp.bfloat16)
    mixed = jnp.dot(activated_b, w_out, preferred_element_type=jnp.float32)
    cotan = upstream.reshape(-1, channels).astype(jnp.float32)
    scale_grad = jnp.sum(cotan * mixed, 0)
    branch = (cotan * layer_scale).astype(jnp.bfloat16)
    out_grad = jnp.dot(activated_b.T, branch, preferred_element_type=jnp.float32)
    hidden_grad = gelu_back(jnp.dot(branch, w_out.T, preferred_element_type=jnp.float32))[0].astype(
        jnp.bfloat16
    )
    in_grad = jnp.dot(scaled.T, hidden_grad, preferred_element_type=jnp.float32)
    normed_grad = jnp.dot(hidden_grad, w_in.T, preferred_element_type=jnp.float32)
    gain_grad = jnp.sum(normed_grad * normed, 0)
    conv_grad_b = norm_backward(normed_grad * norm_gain, normed, inverse).astype(jnp.bfloat16)
    return (conv_grad_b.reshape(conv_out.shape), (gain_grad, in_grad, out_grad, scale_grad))


def body(activations, cotangent, conv_weight, norm_gain, w_in, w_out, layer_scale, neighbours):
    own_block = activations[0]
    upstream = cotangent[0]
    entries = neighbours[0, 0]
    row_total, column_total, channels = own_block.shape
    border_width = DILATION_STEP
    slab_total = lax.axis_size("slab")
    face_total = lax.axis_size("face")
    bands_list = jnp.stack(
        [own_block[:, :border_width], jnp.flip(own_block[:, column_total - border_width :], 1)], 0
    )
    crossed = bands_list
    for bit_index in range(slab_total.bit_length() - 1):
        crossed = from_partner(crossed, "slab", bit_index)
    versions = jnp.stack([bands_list, jnp.flip(crossed, 1)], 0)
    every_face = lax.all_gather(versions[None], "face", axis=0, tiled=True)
    left_band = every_face[entries[0, 0], entries[0, 3], entries[0, 2]]
    right_band = every_face[entries[1, 0], entries[1, 3], entries[1, 2]]
    widened = jnp.concatenate([jnp.flip(left_band, 1), own_block, right_band], 1)
    padded_input = padded(widened, (("slab", 0),), border_width)
    conv_out = dilated(conv_weight, padded_input)
    conv_grad_b, mlp_grads = mlp_pass(conv_out, upstream, norm_gain, w_in, w_out, layer_scale)
    tap_grads = []
    for row_offset in range(3):
        for column_offset in range(3):
            sliding_view = padded_input[
                row_offset * border_width : row_offset * border_width + row_total,
                column_offset * border_width : column_offset * border_width + column_total,
            ]
            tap_grads.append(
                jnp.einsum(
                    "rcn,rcn->n", sliding_view, conv_grad_b, preferred_element_type=jnp.float32
                )
            )
    tap_grad = jnp.stack(tap_grads, 0)
    wide_cols = column_total + 2 * border_width
    zero_padded = jnp.pad(
        conv_grad_b,
        ((2 * border_width, 2 * border_width), (2 * border_width, 2 * border_width), (0, 0)),
    )
    frame_grad = transposed(conv_weight, zero_padded, row_total + 2 * border_width, wide_cols)
    from_below = from_behind(frame_grad[:border_width].astype(jnp.bfloat16), "slab", -1).astype(
        jnp.float32
    )
    from_above = from_behind(
        frame_grad[row_total + border_width :].astype(jnp.bfloat16), "slab", 1
    ).astype(jnp.float32)
    broadened_gradient = frame_grad[border_width : row_total + border_width]
    broadened_gradient = broadened_gradient.at[:border_width].add(from_above)
    broadened_gradient = broadened_gradient.at[row_total - border_width :].add(from_below)
    left_junction = jnp.flip(broadened_gradient[:, :border_width], 1)
    right_junction = broadened_gradient[:, column_total + border_width :]
    outgoing = jnp.zeros((face_total, 2, 2, row_total, border_width, channels), jnp.float32)
    outgoing = outgoing.at[entries[0, 0], entries[0, 3], entries[0, 2]].add(left_junction)
    outgoing = outgoing.at[entries[1, 0], entries[1, 3], entries[1, 2]].add(right_junction)
    incoming = lax.psum_scatter(
        outgoing.astype(jnp.bfloat16), "face", scatter_dimension=0, tiled=True
    ).astype(jnp.float32)[0]
    returned = jnp.flip(incoming[1], 1)
    for bit_index in range(slab_total.bit_length() - 1):
        returned = from_partner(returned, "slab", bit_index)
    edge_grad = incoming[0] + returned
    input_gradient = (
        upstream.astype(jnp.float32)
        + broadened_gradient[:, border_width : column_total + border_width]
    )
    input_gradient = input_gradient.at[:, :border_width].add(edge_grad[0])
    input_gradient = input_gradient.at[:, column_total - border_width :].add(
        jnp.flip(edge_grad[1], 1)
    )
    conv_sum, gain_sum, in_sum, out_sum, scale_sum = lax.psum(
        (tap_grad,) + mlp_grads, ("face", "slab")
    )
    factor = float(row_total * column_total * face_total * slab_total) ** (-0.5)
    return (
        input_gradient.astype(jnp.bfloat16)[None],
        conv_sum * factor,
        gain_sum * factor,
        in_sum * factor,
        out_sum * factor,
        scale_sum * factor,
    )


def solution(mesh):
    return jax.shard_map(
        body,
        mesh=mesh,
        in_specs=(
            P("face", "slab", None, None),
            P("face", "slab", None, None),
            P(),
            P(),
            P(),
            P(),
            P(),
            P("face", "slab", None, None),
        ),
        out_specs=(P("face", "slab", None, None), P(), P(), P(), P(), P()),
        check_vma=False,
    )
```

profile of v0, /device:TPU:1, one launch (start us, length us, event | category | flops | bytes accessed | tf_op | source)
XLA Modules:
  0.0 523.6 jit_solution(12235844592123296284)
XLA Ops:
  8.1 2.0 copy.115
  10.1 3.3 collective-permute-start
  16.8 1.6 collective-permute-start.2
  20.2 5.2 collective-permute-start.3
  39.6 28.3 %all-gather = bf16[16,2,8,2,128]{4,2,3,1,0:T(8,128)(2,1)S(1)} all-gather(bf16[2,2,8,2,128]{4,2,3,1,0:T(8,128)(2,1)S(1)} %pad_maximum_fusion.6), channel_id=2, replica_groups=mesh['face'=8,'slab'=32] {'face'}, dimensions={0}, use_global_device_ids=true | all-gather | bytes 147456 | tf_op jit(solution)/shard_map/all_gather | solution.py:120
  68.3 12.5 %collective-permute-start.5 = (bf16[2,516,128]{2,0,1:T(2,128)(2,1)S(1)}, bf16[2,516,128]{2,0,1:T(2,128)(2,1)S(1)}, u32[]{:S(2)}, u32[]{:S(2)}) collective-permute-start(bf16[2,516,128]{2,0,1:T(2,128)(2,1)S(1)} %get-tuple-element.138), channel_id=1, source_target_pairs={{0,1},{1,2},{2,3},{3,4},{4,5},{5,6},{6,7},{7,8},{8,9},{9,10},{10,1... | collective-permute-start | bytes 792584 | tf_op jit(solution)/shard_map/ppermute | solution.py:28
  80.8 2.4 collective-permute-start.6
  83.9 2.2 fusion.20
  86.1 2.4 collective-permute-done.6
  88.5 2.7 maximum_maximum_fusion
  91.3 4.8 bitcast_convert_fusion.2
  96.1 6.6 %fusion.32 = (f32[8,512]{0,1:T(8,128)S(1)}, f32[8,512,128]{2,0,1:T(8,128)}) fusion(bf16[10,516,128]{2,0,1:T(8,128)(2,1)S(1)} %get-tuple-element.137, f32[128]{0:T(128)S(1)} %copy-done.27, f32[128]{0:T(128)S(1)} %copy-done.29, f32[128]{0:T(128)S(1)} %get-tuple-element.149, bf16[8,2,128]{2,0,1:T(8,128)(2,1)S(1)} %get-tuple-element.145, ...), kind=kLoop, calls=%fused_computation.125 | loop fusion | flops 15200256 | bytes 9466368 | tf_op jit(solution)/shard_map/reduce_sum | solution.py:81
  103.0 3.5 copy.40
  106.5 1.6 multiply_reduce_fusion.3
  108.2 3.7 multiply_convert_fusion.2
  112.0 21.2 %multiply_convert_fusion = (bf16[4096,512]{1,0:T(8,128)(2,1)S(1)}, f32[4096,512]{1,0:T(8,128)}, f32[4096,512]{1,0:T(8,128)}) fusion(bf16[4096,128]{1,0:T(8,128)(2,1)S(1)} %multiply_convert_fusion.2, bf16[128,512]{1,0:T(8,128)(2,1)S(1)} %copy-done), kind=kOutput, calls=%fused_computation.2 | convolution fusion | flops 673185792 | bytes 22151168 | tf_op jit(solution)/shard_map/dot_general | solution.py:87
  133.2 2.0 fusion.36
  135.1 8.0 %add_convert_fusion = bf16[4096,512]{1,0:T(8,128)(2,1)S(1)} fusion(f32[4096,512]{1,0:T(8,128)} %get-tuple-element.121, f32[4096,512]{1,0:T(8,128)} %get-tuple-element.165, bf16[4096,128]{1,0:T(8,128)(2,1)S(1)} %copy-done.14, bf16[512,128]{1,0:T(8,128)(2,1)S(1)} %copy-done.15), kind=kOutput, calls=%fused_computation.3 | convolution fusion | flops 566231040 | bytes 22151168 | tf_op jit(solution)/shard_map/dot_general | solution.py:95
  143.1 2.3 multiply_reduce_fusion.1
  146.8 3.6 bitcast_convert_fusion.6
  151.2 4.1 fusion.31
  157.4 2.0 collective-permute-start.7
  159.5 2.4 collective-permute-start.8
  162.0 4.7 fusion.13
  168.2 2.1 fusion.22
  173.2 3.6 multiply_reduce_fusion
  176.9 79.6 %all-reduce.1 = (f32[9,128]{1,0:T(8,128)S(1)}, f32[128]{0:T(128)S(1)}, f32[128]{0:T(128)S(1)}) all-reduce(f32[9,128]{1,0:T(8,128)S(1)} %stack.63, f32[128]{0:T(128)S(1)} %get-tuple-element.102, f32[128]{0:T(128)S(1)} %fusion.16), channel_id=1, replica_groups=mesh['face'=8,'slab'=32] {'face','slab'}, use_global_device_ids=true, to_apply=%region_7.8 | all-reduce | flops 1408 | bytes 11264 | tf_op jit(solution)/shard_map/psum | solution.py:175
  260.2 1.9 collective-permute-done.10
  262.9 240.8 %all-reduce.5.cloned.1.call-done = (f32[128,512]{1,0:T(8,128)}, f32[512,128]{1,0:T(8,128)}) async-done(((f32[128,512]{1,0:T(8,128)}, f32[512,128]{1,0:T(8,128)}), (f32[128,512]{1,0:T(8,128)}, f32[512,128]{1,0:T(8,128)})) %all-reduce.5.cloned.1.call-update) | async-done | bytes 524304 | tf_op jit(solution)/shard_map/psum | solution.py:175
  503.7 1.7 broadcast_multiply_fusion
  505.4 4.7 collective-permute-start.12
  510.1 1.7 broadcast_multiply_fusion.1
  (142 shorter events, 27.0 us)
Async XLA Ops:
  8.0 103.9 %copy-start = (bf16[128,512]{1,0:T(8,128)(2,1)S(1)}, bf16[128,512]{1,0:T(8,128)(2,1)}, u32[]{:S(2)}) copy-start(bf16[128,512]{1,0:T(8,128)(2,1)} %param.24) | copy-start | bytes 393220
  8.0 6.2 %copy-start.12 = (bf16[1,8,512,128]{3,2,1,0:T(8,128)(2,1)S(1)}, bf16[1,8,512,128]{3,2,1,0:T(8,128)(2,1)}, u32[]{:S(2)}) copy-start(bf16[1,8,512,128]{3,2,1,0:T(8,128)(2,1)} %param.21) | copy-start | bytes 3145732
  8.0 249.1 %reduce-scatter.2.cloned.1.call-start = ((), (), s32[]{:S(2)}) async-start(), calls=%async_computation.1 | async-start | bytes 147456 | tf_op jit(solution)/shard_map/reduce_scatter | solution.py:160
  10.1 4.2 collective-permute-start
  14.3 2.5 collective-permute-start.1
  15.3 10.0 %copy-start.31 = (f32[9,128]{1,0:T(8,128)S(1)}, f32[9,128]{1,0:T(8,128)}, u32[]{:S(2)}) copy-start(f32[9,128]{1,0:T(8,128)} %param.22) | copy-start | bytes 13828
  15.3 12.3 %copy-start.16 = (s32[1,1,2,4]{3,2,1,0:T(2,128)S(1)}, s32[1,1,2,4]{3,2,1,0:T(2,128)}, u32[]{:S(2)}) copy-start(s32[1,1,2,4]{3,2,1,0:T(2,128)} %param.27) | copy-start | bytes 100
  15.3 67.8 %copy-start.33 = (s32[6]{0:T(128)S(1)}, s32[6]{0:T(128)}, u32[]{:S(2)}) copy-start(s32[6]{0:T(128)} %constant.232.clone.1) | copy-start | bytes 76
  16.8 3.4 collective-permute-start.2
  20.2 6.4 %collective-permute-start.3 = (bf16[2,8,2,128]{3,1,2,0:T(8,128)(2,1)S(1)}, bf16[2,8,2,128]{3,1,2,0:T(8,128)(2,1)S(1)}, u32[]{:S(2)}, u32[]{:S(2)}) collective-permute-start(bf16[2,8,2,128]{3,1,2,0:T(8,128)(2,1)S(1)} %collective-permute-done.2), channel_id=1, source_target_pairs={{0,8},{1,9},{2,10},{3,11},{4,12},{5,13},{6,14},{7,15},{8,0},{9,1},... | collective-permute-start | bytes 24584 | tf_op jit(solution)/shard_map/ppermute | solution.py:17
  26.6 13.0 %collective-permute-start.4 = (bf16[2,8,2,128]{3,1,2,0:T(8,128)(2,1)S(1)}, bf16[2,8,2,128]{3,1,2,0:T(8,128)(2,1)S(1)}, u32[]{:S(2)}, u32[]{:S(2)}) collective-permute-start(bf16[2,8,2,128]{3,1,2,0:T(8,128)(2,1)S(1)} %collective-permute-done.3), channel_id=1, source_target_pairs={{0,16},{1,17},{2,18},{3,19},{4,20},{5,21},{6,22},{7,23},{8,24},{9,... | collective-permute-start | bytes 24584 | tf_op jit(solution)/shard_map/ppermute | solution.py:17
  68.3 17.8 %collective-permute-start.5 = (bf16[2,516,128]{2,0,1:T(2,128)(2,1)S(1)}, bf16[2,516,128]{2,0,1:T(2,128)(2,1)S(1)}, u32[]{:S(2)}, u32[]{:S(2)}) collective-permute-start(bf16[2,516,128]{2,0,1:T(2,128)(2,1)S(1)} %get-tuple-element.138), channel_id=1, source_target_pairs={{0,1},{1,2},{2,3},{3,4},{4,5},{5,6},{6,7},{7,8},{8,9},{9,10},{10,1... | collective-permute-start | bytes 792584 | tf_op jit(solution)/shard_map/ppermute | solution.py:28
  80.8 7.7 %collective-permute-start.6 = (bf16[2,516,128]{2,0,1:T(2,128)(2,1)S(1)}, bf16[2,516,128]{2,0,1:T(2,128)(2,1)S(1)}, u32[]{:S(2)}, u32[]{:S(2)}) collective-permute-start(bf16[2,516,128]{2,0,1:T(2,128)(2,1)S(1)} %get-tuple-element.139), channel_id=1, source_target_pairs={{1,0},{2,1},{3,2},{4,3},{5,4},{6,5},{7,6},{8,7},{9,8},{10,9},{11,1... | collective-permute-start | bytes 792584 | tf_op jit(solution)/shard_map/ppermute | solution.py:30
  111.9 21.2 %copy-start.14 = (bf16[4096,128]{1,0:T(8,128)(2,1)S(1)}, bf16[4096,128]{1,0:T(8,128)(2,1)}, u32[]{:S(2)}) copy-start(bf16[4096,128]{1,0:T(8,128)(2,1)} %fusion.14) | copy-start | bytes 3145732
  135.1 8.0 %copy-start.1 = (f32[8,512,128]{2,1,0:T(8,128)S(1)}, f32[8,512,128]{2,1,0:T(8,128)}, u32[]{:S(2)}) copy-start(f32[8,512,128]{2,1,0:T(8,128)} %copy.40) | copy-start | bytes 6291460
  146.8 15.1 %copy-start.10 = (f32[128,512,8]{0,2,1:T(8,128)S(1)}, f32[128,512,8]{0,2,1:T(8,128)}, u32[]{:S(2)}) copy-start(f32[128,512,8]{0,2,1:T(8,128)} %get-tuple-element.168) | copy-start | bytes 6291460
  146.8 15.1 %copy-start.11 = (f32[128,512,8]{0,2,1:T(8,128)S(1)}, f32[128,512,8]{0,2,1:T(8,128)}, u32[]{:S(2)}) copy-start(f32[128,512,8]{0,2,1:T(8,128)} %get-tuple-element.169) | copy-start | bytes 6291460
  151.1 10.8 %copy-start.6 = (f32[128,512,8]{0,2,1:T(8,128)S(1)}, f32[128,512,8]{0,2,1:T(8,128)}, u32[]{:S(2)}) copy-start(f32[128,512,8]{0,2,1:T(8,128)} %get-tuple-element.131) | copy-start | bytes 6291460
  151.1 10.8 %copy-start.7 = (f32[128,512,8]{0,2,1:T(8,128)S(1)}, f32[128,512,8]{0,2,1:T(8,128)}, u32[]{:S(2)}) copy-start(f32[128,512,8]{0,2,1:T(8,128)} %get-tuple-element.132) | copy-start | bytes 6291460
  151.1 10.8 %copy-start.8 = (f32[128,512,8]{0,2,1:T(8,128)S(1)}, f32[128,512,8]{0,2,1:T(8,128)}, u32[]{:S(2)}) copy-start(f32[128,512,8]{0,2,1:T(8,128)} %get-tuple-element.133) | copy-start | bytes 6291460
  151.1 10.8 %copy-start.9 = (f32[128,512,8]{0,2,1:T(8,128)S(1)}, f32[128,512,8]{0,2,1:T(8,128)}, u32[]{:S(2)}) copy-start(f32[128,512,8]{0,2,1:T(8,128)} %get-tuple-element.167) | copy-start | bytes 6291460
  155.3 6.7 %copy-start.4 = (f32[128,512,8]{0,2,1:T(8,128)S(1)}, f32[128,512,8]{0,2,1:T(8,128)}, u32[]{:S(2)}) copy-start(f32[128,512,8]{0,2,1:T(8,128)} %get-tuple-element.140) | copy-start | bytes 6291460
  155.3 6.7 %copy-start.5 = (f32[128,512,8]{0,2,1:T(8,128)S(1)}, f32[128,512,8]{0,2,1:T(8,128)}, u32[]{:S(2)}) copy-start(f32[128,512,8]{0,2,1:T(8,128)} %get-tuple-element.141) | copy-start | bytes 6291460
  157.4 10.8 %collective-permute-start.7 = (bf16[2,516,128]{2,0,1:T(2,128)(2,1)S(1)}, bf16[2,516,128]{2,0,1:T(2,128)(2,1)S(1)}, u32[]{:S(2)}, u32[]{:S(2)}) collective-permute-start(bf16[2,516,128]{2,0,1:T(2,128)(2,1)S(1)} %get-tuple-element.135), channel_id=1, source_target_pairs={{0,1},{1,2},{2,3},{3,4},{4,5},{5,6},{6,7},{7,8},{8,9},{9,10},{10,1... | collective-permute-start | bytes 792584 | tf_op jit(solution)/shard_map/ppermute | solution.py:40
  159.5 10.8 %collective-permute-start.8 = (bf16[2,516,128]{2,0,1:T(2,128)(2,1)S(1)}, bf16[2,516,128]{2,0,1:T(2,128)(2,1)S(1)}, u32[]{:S(2)}, u32[]{:S(2)}) collective-permute-start(bf16[2,516,128]{2,0,1:T(2,128)(2,1)S(1)} %get-tuple-element.134), channel_id=1, source_target_pairs={{1,0},{2,1},{3,2},{4,3},{5,4},{6,5},{7,6},{8,7},{9,8},{10,9},{11,1... | collective-permute-start | bytes 792584 | tf_op jit(solution)/shard_map/ppermute | solution.py:40
  173.2 330.5 %all-reduce.5.cloned.1.call-start = ((), (), s32[]{:S(2)}) async-start(), calls=%async_computation.2 | async-start | bytes 1048576 | tf_op jit(solution)/shard_map/psum | solution.py:175
  173.2 339.8 %copy-start.13 = (bf16[1,8,512,128]{3,2,1,0:T(8,128)(2,1)S(1)}, bf16[1,8,512,128]{3,2,1,0:T(8,128)(2,1)}, u32[]{:S(2)}) copy-start(bf16[1,8,512,128]{3,2,1,0:T(8,128)(2,1)} %param.21) | copy-start | bytes 3145732
  257.9 1.6 collective-permute-start.9
  259.5 2.6 collective-permute-start.10
  262.1 243.3 %collective-permute-start.11 = (f32[2,8,2,128]{3,1,2,0:T(8,128)S(1)}, f32[2,8,2,128]{3,1,2,0:T(8,128)S(1)}, u32[]{:S(2)}, u32[]{:S(2)}) collective-permute-start(f32[2,8,2,128]{3,1,2,0:T(8,128)S(1)} %collective-permute-done.10), channel_id=1, source_target_pairs={{0,4},{1,5},{2,6},{3,7},{4,0},{5,1},{6,2},{7,3},{8,12},{9,13},{10,... | collective-permute-start | bytes 49160 | tf_op jit(solution)/shard_map/ppermute | solution.py:17
  505.4 6.5 %collective-permute-start.12 = (f32[2,8,2,128]{3,1,2,0:T(8,128)S(1)}, f32[2,8,2,128]{3,1,2,0:T(8,128)S(1)}, u32[]{:S(2)}, u32[]{:S(2)}) collective-permute-start(f32[2,8,2,128]{3,1,2,0:T(8,128)S(1)} %collective-permute-done.11), channel_id=1, source_target_pairs={{0,8},{1,9},{2,10},{3,11},{4,12},{5,13},{6,14},{7,15},{8,0},{9,1},... | collective-permute-start | bytes 49160 | tf_op jit(solution)/shard_map/ppermute | solution.py:17
  511.9 2.8 collective-permute-start.13
  (19 other events, 77.2 us)
Sparse Core Ops, SparseCore 0:
  173.3 75.8 reduce-scatter.1
Sparse Core Ops, SparseCore 1:
  257.2 246.4 all-reduce.4
where the time goes:
time: 532 us; the launch traced here: 524 us
  waiting for transfers between devices  250 us (47%)
  blocking collectives  108 us (20%)
  other arithmetic  51.8 us (10%)
  starting transfers between devices  38.1 us (7%)
  matrix products  36.1 us (7%)
  between operations  27.6 us (5%)
  local copies, waits for them, and re-layouts  11.8 us (2%)
    psum x1, waiting for transfers between devices, body(): lax.psum((tap_grad,) + mlp_grads, ('face', 'slab'))  241 us
    psum x1, blocking collectives, body(): lax.psum((tap_grad,) + mlp_grads, ('face', 'slab'))  79.6 us
    all_gather x1, blocking collectives, body(): every_face = lax.all_gather(versions[None], 'face', axis=0, tiled=True)  28.3 us
    dot_general x1, matrix products, mlp_pass(): hidden = jnp.dot(scaled, w_in, preferred_element_type=jnp.float32)  21.2 us
    ppermute x10, starting transfers between devices, from_partner(): return lax.ppermute(value, axis, pairs)  18.7 us
    ppermute x1, starting transfers between devices, padded(): lax.ppermute(tail, axis, [(i, (i + 1) % count) for i in range(ends)])  12.5 us
  transfers between devices with their start and end apart: 16, of which 10 were waited for; matrix products, arithmetic and copies ran while one was open for 5% of the time, Pallas kernels for 0%

commit v1 on v0

v1 whole, which is shorter than its diff:
```python
import math
from functools import partial

import jax
import jax.numpy as jnp
from jax import lax
from jax.experimental import pallas as pl
from jax.experimental.pallas import tpu as pltpu
from jax.sharding import PartitionSpec as P

F32, BF16 = jnp.float32, jnp.bfloat16
FACES, SLABS = 8, 32
DEPTH = 8
PLANE = 32
ROWS, COLS, CH, HID = 8, 512, 128, 512
PAD = 8
WIDE = COLS + 2 * PAD
CHUNK = 128
SHARE = 32
CELLS = FACES * SLABS * ROWS * COLS
FACTOR = float(CELLS) ** (-0.5)
EPSILON = 1e-6
SQRT_HALF = math.sqrt(0.5)
EXPONENT = -math.log2(math.e)
BIAS = math.log2(2 / math.sqrt(2 * math.pi))
MESH = pl.DeviceIdType.MESH


def dot(a, b, dims=((1,), (0,))):
    return lax.dot_general(a, b, (dims, ((), ())), preferred_element_type=F32)


def prepare(wi, wo, gain, scale, wd_ref, wn_ref):
    wd_ref[...] = (wo.astype(F32) * (0.5 * scale)).T.astype(BF16)
    wit = wi.astype(F32).T
    wn_ref[:, :CH] = wit.astype(BF16)
    mean = jnp.mean(wit * gain, -1, keepdims=True)
    wn_ref[:, CH:] = jnp.broadcast_to(mean, (HID, CH)).astype(BF16)


def row_pass(r, cw, gain, xp, cot_ref, wi_ref, wd_ref, wn_ref, sc, nm, iv, hg, ng, gp, gb, og, ig, tg):
    ones = jnp.full((2 * CH, CH), 1 / CH, BF16)
    for c0 in range(0, COLS, CHUNK):
        acc = None
        for i in range(3):
            for j in range(3):
                t = cw[3 * i + j : 3 * i + j + 1] * xp[r + 2 * i, pl.ds(PAD - 2 + 2 * j + c0, CHUNK), :]
                acc = t if acc is None else acc + t
        hi = acc.astype(BF16)
        lo = (acc - hi.astype(F32)).astype(BF16)
        centred = acc - dot(jnp.concatenate([hi, lo], 1), ones)
        variance = dot((centred * centred).astype(BF16), ones[:CH])
        inverse = lax.rsqrt(variance + EPSILON)
        normed = centred * inverse
        sc[c0 : c0 + CHUNK, :] = (normed * gain).astype(BF16)
        nm[c0 : c0 + CHUNK, :] = normed
        iv[c0 : c0 + CHUNK, :] = inverse
    cot = cot_ref[0, r]
    scaled = sc[...]
    for n0 in range(0, HID, 256):
        hidden = dot(scaled, wi_ref[:, n0 : n0 + 256])
        upstream = dot(cot, wd_ref[:, n0 : n0 + 256])
        x = hidden * SQRT_HALF
        twice = 1.0 + lax.erf(x)
        activated = (hidden * twice).astype(BF16)
        density = jnp.exp2(x * x * EXPONENT + BIAS)
        hidden_grad = ((twice + hidden * density) * upstream).astype(BF16)
        hg[:, n0 : n0 + 256] = hidden_grad
        og[:, n0 : n0 + 256] += dot(cot, activated, ((0,), (0,)))
        ig[:, n0 : n0 + 256] += dot(scaled, hidden_grad, ((0,), (0,)))
    ng[...] = dot(hg[...], wn_ref[...])
    for c0 in range(0, COLS, CHUNK):
        d = ng[c0 : c0 + CHUNK, :CH] * gain
        d_mean = ng[c0 : c0 + CHUNK, CH:]
        normed = nm[c0 : c0 + CHUNK, :]
        dn_mean = dot((d * normed).astype(BF16), ones[:CH])
        gb16 = (iv[c0 : c0 + CHUNK, :] * (d - d_mean - normed * dn_mean)).astype(BF16)
        gb[r, c0 : c0 + CHUNK, :] = gb16
        g = gb16.astype(F32)
        gp[r + 2, PAD + c0 : PAD + c0 + CHUNK, :] = g
        for i in range(3):
            for j in range(3):
                t = g * xp[r + 2 * i, pl.ds(PAD - 2 + 2 * j + c0, CHUNK), :]
                tg[3 * i + j] += t.reshape(CHUNK // 8, 8, CH).sum(0)


def transposed_row(r, cw, gp, cot_ref, dx, edge):
    for c0 in range(0, COLS, CHUNK):
        acc = cot_ref[0, r, c0 : c0 + CHUNK, :].astype(F32)
        for i in range(3):
            for j in range(3):
                acc = acc + cw[3 * i + j : 3 * i + j + 1] * gp[r + 4 - 2 * i, pl.ds(PAD + 2 - 2 * j + c0, CHUNK), :]
        dx[0, r, c0 : c0 + CHUNK, :] = acc.astype(BF16)
        if c0 == 0:
            edge[0, r] = acc[:16]
        if c0 == COLS - CHUNK:
            edge[1, r] = acc[CHUNK - 16 :]


def kernel(
    act, cot, cw_ref, gain_ref, wi, wo, scale_ref, nb,
    dx, o_conv, o_gain, o_in, o_out, o_scale,
    xp, gp, wd, wn, sc, nm, iv, hg, ng, gb, og, ig, tg, edge,
    bands, gathered, stage, picked, corner_out, corner_in, halo, ghalo, strips, returned,
    big, small, part1, smallz, c2, part2, smalla, s2, c3, part3,
    seam_s, seam_r, ret_s, ret_r, near_s, near_r, one_s, one_r, two_s, two_r, three_s, three_r, za_s, za_r, zb_s, zb_r,
):
    f, s = lax.axis_index("face"), lax.axis_index("slab")
    x_lo, z, core = s // 16, (s // 2) % DEPTH, s % 2
    a = f * 4 + x_lo * 2 + core
    mirror = SLABS - 1 - s
    up, down = (s + SLABS - 1) % SLABS, (s + 1) % SLABS

    def in_plane(j):
        other = (a + j) % PLANE
        return other, (other // 4, ((other // 2) % 2) * 16 + z * 2 + other % 2)

    def in_depth(j):
        other = (z + j) % DEPTH
        return other, (f, x_lo * 16 + other * 2 + core)

    def loop(low, high, step):
        def body(j, carry):
            step(j)
            return carry

        lax.fori_loop(low, high, body, 0)

    barrier = pltpu.get_barrier_semaphore()

    def greet(device):
        pl.semaphore_signal(barrier, inc=1, device_id=device, device_id_type=MESH)

    greet((f, up))
    greet((f, down))
    loop(0, FACES, lambda j: greet(((f + j) % FACES, mirror)))
    loop(1, PLANE, lambda j: greet(in_plane(j)[1]))
    loop(1, DEPTH, lambda j: greet(in_depth(j)[1]))

    for r in range(ROWS):
        left = act[0, r, 0:16, :].astype(F32)
        right = act[0, r, COLS - 16 : COLS, :].astype(F32)
        for q in range(2):
            stage[0, q * 8 + r : q * 8 + r + 1, :] = left[q : q + 1]
            stage[1, q * 8 + r : q * 8 + r + 1, :] = right[15 - q : 16 - q]
    bands[...] = stage[...].astype(BF16)
    gathered[0, f] = bands[...]

    pl.semaphore_wait(barrier, 2 + FACES + PLANE - 1 + DEPTH - 1)

    def copy(src, dst, send, recv, device):
        return pltpu.make_async_remote_copy(
            src_ref=src, dst_ref=dst, send_sem=send, recv_sem=recv, device_id=device, device_id_type=MESH
        )

    def seam_copy(src, dst, sends, recvs, k, j):
        device = ((f + j) % FACES, mirror if k else s)
        return copy(src, dst.at[k, f], sends.at[k * FACES + j], recvs.at[k * FACES + f], device)

    def seam_start(src, dst, sends, recvs):
        loop(1, FACES, lambda j: seam_copy(src, dst, sends, recvs, 0, j).start())
        loop(0, FACES, lambda j: seam_copy(src, dst, sends, recvs, 1, j).start())

    def seam_wait(src, dst, sends, recvs):
        def arrived(k, j):
            face = (f + j) % FACES
            copy(src, dst.at[k, face], sends.at[k * FACES + j], recvs.at[k * FACES + face], (face, s)).wait_recv()

        loop(1, FACES, lambda j: arrived(0, j))
        loop(0, FACES, lambda j: arrived(1, j))

    def seam_sent(src, dst, sends, recvs):
        loop(1, FACES, lambda j: seam_copy(src, dst, sends, recvs, 0, j).wait_send())
        loop(0, FACES, lambda j: seam_copy(src, dst, sends, recvs, 1, j).wait_send())

    def pick(src):
        out = []
        for e in range(2):
            sf, se, k = nb[0, 0, e, 0], nb[0, 0, e, 2], nb[0, 0, e, 3]
            picked[e] = src[k, sf, se].astype(F32)
            out.append([
                [jnp.where(k == 1, picked[e, q * 8 + 7 - r : q * 8 + 8 - r, :], picked[e, q * 8 + r : q * 8 + r + 1, :]) for r in range(ROWS)]
                for q in range(2)
            ])
        return out

    halo_up = copy(act.at[0, pl.ds(0, 2)], halo.at[1], near_s.at[0], near_r.at[1], (f, up))
    halo_down = copy(act.at[0, pl.ds(ROWS - 2, 2)], halo.at[0], near_s.at[1], near_r.at[0], (f, down))
    corner_up = copy(corner_out.at[0], corner_in.at[1], near_s.at[2], near_r.at[3], (f, up))
    corner_down = copy(corner_out.at[1], corner_in.at[0], near_s.at[3], near_r.at[2], (f, down))
    grad_up = copy(gb.at[pl.ds(0, 2)], ghalo.at[1], near_s.at[4], near_r.at[5], (f, up))
    grad_down = copy(gb.at[pl.ds(ROWS - 2, 2)], ghalo.at[0], near_s.at[5], near_r.at[4], (f, down))

    seam_start(bands, gathered, seam_s, seam_r)
    halo_up.start()
    halo_down.start()

    gain, scale = gain_ref[...], scale_ref[...]
    cw = cw_ref[...]
    prepare(wi[...], wo[...], gain, scale, wd, wn)
    og[...] = jnp.zeros_like(og)
    ig[...] = jnp.zeros_like(ig)
    tg[...] = jnp.zeros_like(tg)
    for r in range(ROWS + 4):
        gp[r, 0:PAD, :] = jnp.zeros((PAD, CH), F32)
        gp[r, PAD + COLS :, :] = jnp.zeros((PAD, CH), F32)

    def own(r):
        xp[r + 2, PAD : PAD + COLS, :] = act[0, r].astype(F32)

    loop(0, ROWS, own)

    seam_wait(bands, gathered, seam_s, seam_r)
    strip = pick(gathered)
    for r in range(ROWS):
        for q in range(2):
            xp[r + 2, PAD - 1 - q : PAD - q, :] = strip[0][q][r]
            xp[r + 2, PAD + COLS + q : PAD + COLS + q + 1, :] = strip[1][q][r]
    for e in range(2):
        for q in range(2):
            for t in range(2):
                place = e * 4 + q * 2 + t
                corner_out[0, place : place + 1, :] = strip[e][q][t]
                corner_out[1, place : place + 1, :] = strip[e][q][ROWS - 2 + t]
    corner_up.start()
    corner_down.start()

    def rows_of(low, high):
        loop(low, high, lambda r: row_pass(r, cw, gain, xp, cot, wi, wd, wn, sc, nm, iv, hg, ng, gp, gb, og, ig, tg))

    rows_of(2, 6)

    halo_up.wait_recv()
    halo_down.wait_recv()
    corner_up.wait_recv()
    corner_down.wait_recv()
    inside = (jnp.where(s == 0, 0.0, 1.0), jnp.where(s == SLABS - 1, 0.0, 1.0))
    for side in range(2):
        for t in range(2):
            row = t + side * (ROWS + 2)
            xp[row, PAD : PAD + COLS, :] = halo[side, t].astype(F32) * inside[side]
            for q in range(2):
                left, right = q * 2 + t, 4 + q * 2 + t
                xp[row, PAD - 1 - q : PAD - q, :] = corner_in[side, left : left + 1, :] * inside[side]
                xp[row, PAD + COLS + q : PAD + COLS + q + 1, :] = corner_in[side, right : right + 1, :] * inside[side]

    rows_of(0, 2)
    grad_up.start()
    rows_of(ROWS - 2, ROWS)
    grad_down.start()

    products = og[...].T
    out_part = products * (0.5 * FACTOR * scale)
    in_part = ig[...] * FACTOR
    for b in range(HID // SHARE):
        big[b] = out_part[b * SHARE : (b + 1) * SHARE].astype(BF16)
    for b in range(HID // CH):
        for t in range(CH // SHARE):
            big[HID // SHARE + b * (CH // SHARE) + t] = in_part[t * SHARE : (t + 1) * SHARE, b * CH : (b + 1) * CH].astype(BF16)
    small[...] = jnp.zeros_like(small)
    small[0:9, :] = jnp.sum(tg[...], 1) * FACTOR
    in_sum = jnp.sum((in_part * wi[...].astype(F32)).T, 0, keepdims=True)
    small[9:10, :] = in_sum / gain
    small[10:11, :] = jnp.sum(products * wo[...].astype(F32), 0, keepdims=True) * (0.5 * FACTOR)

    def plane_copy(src, dst, sends, recvs, j):
        other, device = in_plane(j)
        return copy(src(other), dst.at[a], sends.at[j], recvs.at[a], device)

    def plane_wait(dst, recvs, j):
        other, device = in_plane(j)
        copy(dst.at[other], dst.at[other], recvs.at[other], recvs.at[other], device).wait_recv()

    def depth_copy(src, dst, sends, recvs, j):
        other, device = in_depth(j)
        return copy(src, dst.at[z], sends.at[j], recvs.at[z], device)

    def depth_wait(dst, recvs, j):
        other, device = in_depth(j)
        copy(dst.at[other], dst.at[other], recvs.at[other], recvs.at[other], device).wait_recv()

    one = partial(plane_copy, lambda other: big.at[other], part1, one_s, one_r)
    two = partial(depth_copy, c2, part2, za_s, za_r)
    three = partial(plane_copy, lambda other: c3, part3, three_s, three_r)
    small_one = partial(depth_copy, small, smallz, zb_s, zb_r)
    small_two = partial(plane_copy, lambda other: s2, smalla, two_s, two_r)

    loop(1, PLANE, lambda j: one(j).start())
    loop(1, DEPTH, lambda j: small_one(j).start())
    part1[a] = big[a]
    smallz[z] = small[...]

    def transposed_rows(low, high):
        loop(low, high, lambda r: transposed_row(r, cw, gp, cot, dx, edge))

    transposed_rows(2, 6)

    grad_up.wait_recv()
    grad_down.wait_recv()
    for side in range(2):
        for t in range(2):
            gp[t + side * (ROWS + 2), PAD : PAD + COLS, :] = ghalo[side, t].astype(F32) * inside[side]
    for r in range(ROWS):
        left, right = jnp.zeros((8, CH), F32), jnp.zeros((8, CH), F32)
        for i in range(3):
            left = left + cw[3 * i : 3 * i + 1] * gp[r + 4 - 2 * i, PAD : PAD + 8, :]
            right = right + cw[3 * i + 2 : 3 * i + 3] * gp[r + 4 - 2 * i, PAD + COLS - 8 : PAD + COLS, :]
        for q in range(2):
            stage[0, q * 8 + r : q * 8 + r + 1, :] = left[1 - q : 2 - q]
            stage[1, q * 8 + r : q * 8 + r + 1, :] = right[6 + q : 7 + q]
    strips[...] = stage[...].astype(BF16)
    returned[0, f] = strips[...]
    seam_start(strips, returned, ret_s, ret_r)

    transposed_rows(0, 2)
    transposed_rows(ROWS - 2, ROWS)

    loop(1, PLANE, lambda j: plane_wait(part1, one_r, j))
    loop(1, DEPTH, lambda j: depth_wait(smallz, zb_r, j))
    total = part1[0].astype(F32)
    for b in range(1, PLANE):
        total = total + part1[b].astype(F32)
    c2[...] = total.astype(BF16)
    s2[...] = jnp.sum(smallz[...], 0)
    part2[z] = c2[...]
    smalla[a] = s2[...]
    loop(1, DEPTH, lambda j: two(j).start())
    loop(1, PLANE, lambda j: small_two(j).start())

    seam_wait(strips, returned, ret_s, ret_r)
    back = pick(returned)
    for r in range(ROWS):
        for q in range(2):
            edge[0, r, q : q + 1, :] += back[0][q][r]
            edge[1, r, 15 - q : 16 - q, :] += back[1][q][r]
        dx[0, r, 0:16, :] = edge[0, r].astype(BF16)
        dx[0, r, COLS - 16 : COLS, :] = edge[1, r].astype(BF16)

    loop(1, DEPTH, lambda j: depth_wait(part2, za_r, j))
    c3[...] = jnp.sum(part2[...].astype(F32), 0).astype(BF16)
    part3[a] = c3[...]
    loop(1, PLANE, lambda j: three(j).start())

    loop(1, PLANE, lambda j: plane_wait(smalla, two_r, j))
    sums = smalla[0]
    for b in range(1, PLANE):
        sums = sums + smalla[b]
    o_conv[...] = sums[0:9]
    o_gain[...] = sums[9:10]
    o_scale[...] = sums[10:11]

    seam_sent(bands, gathered, seam_s, seam_r)
    seam_sent(strips, returned, ret_s, ret_r)
    for sent in (halo_up, halo_down, corner_up, corner_down, grad_up, grad_down):
        sent.wait_send()
    loop(1, PLANE, lambda j: one(j).wait_send())
    loop(1, PLANE, lambda j: small_two(j).wait_send())
    loop(1, DEPTH, lambda j: two(j).wait_send())
    loop(1, DEPTH, lambda j: small_one(j).wait_send())

    loop(1, PLANE, lambda j: plane_wait(part3, three_r, j))
    for b in range(HID // SHARE):
        o_out[b * SHARE : (b + 1) * SHARE, :] = part3[b].astype(F32)
    for b in range(HID // CH):
        for t in range(CH // SHARE):
            o_in[t * SHARE : (t + 1) * SHARE, b * CH : (b + 1) * CH] = part3[HID // SHARE + b * (CH // SHARE) + t].astype(F32)
    loop(1, PLANE, lambda j: three(j).wait_send())


def body(activations, cotangent, conv_weight, norm_gain, w_in, w_out, layer_scale, neighbours):
    vmem = pl.BlockSpec(memory_space=pltpu.VMEM)
    smem = pl.BlockSpec(memory_space=pltpu.SMEM)
    dma = pltpu.SemaphoreType.DMA

    def buf(*shape, dtype=F32):
        return pltpu.VMEM(shape, dtype)

    half = partial(buf, dtype=BF16)
    outs = pl.pallas_call(
        kernel,
        out_shape=[
            jax.ShapeDtypeStruct((1, ROWS, COLS, CH), BF16),
            jax.ShapeDtypeStruct((9, CH), F32),
            jax.ShapeDtypeStruct((1, CH), F32),
            jax.ShapeDtypeStruct((CH, HID), F32),
            jax.ShapeDtypeStruct((HID, CH), F32),
            jax.ShapeDtypeStruct((1, CH), F32),
        ],
        in_specs=[vmem] * 7 + [smem],
        out_specs=[vmem] * 6,
        scratch_shapes=[
            buf(ROWS + 4, WIDE, CH), buf(ROWS + 4, WIDE, CH), half(CH, HID), half(HID, 2 * CH),
            half(COLS, CH), buf(COLS, CH), buf(COLS, CH), half(COLS, HID), buf(COLS, 2 * CH), half(ROWS, COLS, CH),
            buf(CH, HID), buf(CH, HID), buf(9, 8, CH), buf(2, ROWS, 16, CH),
            half(2, 16, CH), half(2, FACES, 2, 16, CH), buf(2, 16, CH), buf(2, 16, CH), buf(2, 8, CH), buf(2, 8, CH),
            half(2, 2, COLS, CH), half(2, 2, COLS, CH), half(2, 16, CH), half(2, FACES, 2, 16, CH),
            half(PLANE, SHARE, CH), buf(16, CH), half(PLANE, SHARE, CH), buf(DEPTH, 16, CH), half(SHARE, CH),
            half(DEPTH, SHARE, CH), buf(PLANE, 16, CH), buf(16, CH), half(SHARE, CH), half(PLANE, SHARE, CH),
            dma((16,)), dma((16,)), dma((16,)), dma((16,)), dma((6,)), dma((6,)),
            dma((PLANE,)), dma((PLANE,)), dma((PLANE,)), dma((PLANE,)), dma((PLANE,)), dma((PLANE,)),
            dma((DEPTH,)), dma((DEPTH,)), dma((DEPTH,)), dma((DEPTH,)),
        ],
        compiler_params=pltpu.CompilerParams(collective_id=0, has_side_effects=True, vmem_limit_bytes=56 * 2**20),
    )(
        activations, cotangent, conv_weight, norm_gain.reshape(1, CH), w_in, w_out, layer_scale.reshape(1, CH), neighbours
    )
    dx, conv_grad, gain_grad, in_grad, out_grad, scale_grad = outs
    return dx, conv_grad, gain_grad.reshape(CH), in_grad, out_grad, scale_grad.reshape(CH)


def solution(mesh):
    cells = P("face", "slab", None, None)
    return jax.shard_map(
        body,
        mesh=mesh,
        in_specs=(cells, cells, P(), P(), P(), P(), P(), cells),
        out_specs=(cells, P(), P(), P(), P(), P()),
        check_vma=False,
    )
```

time: 532 us -> 66.1 us (0.12); the launches traced: 524 us -> 65.9 us
  waiting for transfers between devices: 250 us -> 0 us
  blocking collectives: 108 us -> 0 us
  Pallas kernels: 0 us -> 59.5 us
  other arithmetic: 51.8 us -> 0 us
  starting transfers between devices: 38.1 us -> 0 us
  matrix products: 36.1 us -> 0 us
  between operations: 27.6 us -> 0.67 us
  local copies, waits for them, and re-layouts: 11.8 us -> 5.76 us
    psum x1 -> x0, waiting for transfers between devices: 241 us -> none  [body(): lax.psum((tap_grad,) + mlp_grads, ('face', 'slab'))]
    psum x1 -> x0, blocking collectives: 79.6 us -> none  [body(): lax.psum((tap_grad,) + mlp_grads, ('face', 'slab'))]
    pallas_call x0 -> x1, Pallas kernels: none -> 59.5 us  [body(): pl.pallas_call(kernel, out_shape=[jax.ShapeDtypeStruct((1, ROWS, COLS, CH...]
    ppermute x14 -> x0, starting transfers between devices: 38 us -> none  [the longest x10 18.7 us: from_partner(): return lax.ppermute(value, axis, pairs)]
    dot_general x6 -> x0, matrix products: 36.1 us -> none  [the longest x1 21.2 us: mlp_pass(): hidden = jnp.dot(scaled, w_in, preferred_element_type=jnp.float32)]
    all_gather x1 -> x0, blocking collectives: 28.3 us -> none  [body(): every_face = lax.all_gather(versions[None], 'face', axis=0, tiled=True)]
    unnamed x4 -> x0, other arithmetic: 10.6 us -> none
    ppermute x14 -> x0, waiting for transfers between devices: 9.38 us -> none  [the longest x10 7 us: from_partner(): return lax.ppermute(value, axis, pairs)]
  transfers between devices with their start and end apart: 16 -> 0, of which waited for: 10 -> 0; matrix products, arithmetic and copies ran while one was open for 5% -> 0% of each run, Pallas kernels for 0% -> 0%
where the time goes in v1:
time: 66.1 us; the launch traced here: 65.9 us
  Pallas kernels  59.5 us (90%)
  local copies, waits for them, and re-layouts  5.76 us (9%)
  between operations  0.67 us (1%)
    pallas_call x1, Pallas kernels, body(): pl.pallas_call(kernel, out_shape=[jax.ShapeDtypeStruct((1, ROWS, COLS, CH...  59.5 us
    unnamed x16, local copies, waits for them, and re-layouts  5.76 us

profile of v1, /device:TPU:1, one launch (start us, length us, event | category | flops | bytes accessed | tf_op | source)
XLA Modules:
  0.0 65.9 jit_solution(542423049211816747)
XLA Ops:
  0.6 59.5 %shard_map.127 = (bf16[1,8,512,128]{3,2,1,0:T(8,128)(2,1)}, f32[9,128]{1,0:T(8,128)}, f32[1,128]{1,0:T(1,128)}, f32[128,512]{1,0:T(8,128)}, f32[512,128]{1,0:T(8,128)}, /*index=5*/f32[1,128]{1,0:T(1,128)}) custom-call(bf16[1,8,512,128]{3,2,1,0:T(8,128)(2,1)} %act.1, bf16[1,8,512,128]{3,2,1,0:T(8,128)(2,1)} %cot.1, f32[9,128]{1,0:T(8,128)} %cw_ref.1, ...), custom_call_target="tpu_custom_call" | custom-call | tf_op jit(solution)/shard_map/pallas_call | solution.py:379
  60.1 0.0 copy-start.2
  60.1 0.0 copy-start.1
  60.1 2.3 %copy.20 = bf16[1,8,512,128]{3,2,1,0:T(8,128)(2,1)} copy(bf16[1,8,512,128]{3,2,1,0:T(8,128)(2,1)} %get-tuple-element.24) | data formatting | bytes 2097152
  62.5 0.0 copy-done.2
  62.5 0.0 copy-start.4
  62.5 0.6 copy.21
  63.1 0.1 copy-done.4
  63.1 0.5 copy.22
  63.6 0.0 copy-done.1
  63.6 0.0 copy-start
  63.6 0.7 %copy.23 = f32[128,512]{1,0:T(8,128)} copy(f32[128,512]{1,0:T(8,128)S(1)} %copy-done.1) | data formatting | bytes 524288
  64.3 0.3 copy-done
  64.7 0.0 copy-start.3
  64.7 0.7 %copy.24 = f32[512,128]{1,0:T(8,128)} copy(f32[512,128]{1,0:T(8,128)S(1)} %copy-done) | data formatting | bytes 524288
  65.4 0.0 copy-done.3
  65.4 0.5 copy.25
Async XLA Ops:
  60.1 2.3 %copy-start.2 = (f32[9,128]{1,0:T(8,128)S(1)}, f32[9,128]{1,0:T(8,128)}, u32[]{:S(2)}) copy-start(f32[9,128]{1,0:T(8,128)} %get-tuple-element.25) | copy-start | bytes 13828
  60.1 3.5 %copy-start.1 = (f32[128,512]{1,0:T(8,128)S(1)}, f32[128,512]{1,0:T(8,128)}, u32[]{:S(2)}) copy-start(f32[128,512]{1,0:T(8,128)} %get-tuple-element.27) | copy-start | bytes 786436
  62.5 0.7 %copy-start.4 = (f32[1,128]{1,0:T(1,128)S(1)}, f32[1,128]{1,0:T(1,128)}, u32[]{:S(2)}) copy-start(f32[1,128]{1,0:T(1,128)} %get-tuple-element.14) | copy-start | bytes 1540
  63.6 1.0 %copy-start = (f32[512,128]{1,0:T(8,128)S(1)}, f32[512,128]{1,0:T(8,128)}, u32[]{:S(2)}) copy-start(f32[512,128]{1,0:T(8,128)} %get-tuple-element.28) | copy-start | bytes 786436
  64.7 0.7 %copy-start.3 = (f32[1,128]{1,0:T(1,128)S(1)}, f32[1,128]{1,0:T(1,128)}, u32[]{:S(2)}) copy-start(f32[1,128]{1,0:T(1,128)} %get-tuple-element.17) | copy-start | bytes 1540

commit v2 on v1

v2 whole, which is shorter than its diff:
```python
import math
from functools import partial

import jax
import jax.numpy as jnp
from jax import lax
from jax.experimental import pallas as pl
from jax.experimental.pallas import tpu as pltpu
from jax.sharding import PartitionSpec as P

F32, BF16 = jnp.float32, jnp.bfloat16
FACES, SLABS = 8, 32
DEPTH = 8
PLANE = 32
ROWS, COLS, CH, HID = 8, 512, 128, 512
PAD = 8
WIDE = COLS + 2 * PAD
CHUNK = 64
SHARE = 32
CELLS = FACES * SLABS * ROWS * COLS
FACTOR = float(CELLS) ** (-0.5)
EPSILON = 1e-6
SQRT_HALF = math.sqrt(0.5)
EXPONENT = -math.log2(math.e)
BIAS = math.log2(2 / math.sqrt(2 * math.pi))
MESH = pl.DeviceIdType.MESH


def dot(a, b, dims=((1,), (0,))):
    return lax.dot_general(a, b, (dims, ((), ())), preferred_element_type=F32)


def prepare(wi, wo, scale, wd_ref, wn_ref):
    wd_ref[...] = (wo.astype(F32) * (0.5 * scale)).T.astype(BF16)
    wn_ref[...] = wi.astype(F32).T.astype(BF16)


def forward(pieces, size, cw, gain, xp, cv, wi_ref, wd_ref, sc, nm, iv, hg, og, ig):
    total = len(pieces) * size
    for n, (r, c0) in enumerate(pieces):
        acc = None
        for i in range(3):
            for j in range(3):
                t = cw[3 * i + j : 3 * i + j + 1] * xp[r + 2 * i, pl.ds(PAD - 2 + 2 * j + c0, size), :]
                acc = t if acc is None else acc + t
        centred = acc - jnp.mean(acc, -1, keepdims=True)
        variance = jnp.mean(centred * centred, -1, keepdims=True)
        inverse = jnp.broadcast_to(lax.rsqrt(variance + EPSILON), (size, CH))
        normed = centred * inverse
        sc[n * size : (n + 1) * size, :] = (normed * gain).astype(BF16)
        nm[r, c0 : c0 + size, :] = normed
        iv[r, c0 : c0 + size, :] = inverse
    cot = jnp.concatenate([cv[r, c0 : c0 + size, :] for r, c0 in pieces], 0)
    scaled = sc[:total, :]
    hidden = dot(scaled, wi_ref[...])
    upstream = dot(cot, wd_ref[...])
    x = hidden * SQRT_HALF
    twice = 1.0 + lax.erf(x)
    activated = (hidden * twice).astype(BF16)
    density = jnp.exp2(x * x * EXPONENT + BIAS)
    hidden_grad = ((twice + hidden * density) * upstream).astype(BF16)
    for n, (r, c0) in enumerate(pieces):
        hg[r, c0 : c0 + size, :] = hidden_grad[n * size : (n + 1) * size]
    og[...] += dot(cot, activated, ((0,), (0,)))
    ig[...] += dot(scaled, hidden_grad, ((0,), (0,)))


def backward(r, gain, xp, wn_ref, nm, iv, hg, ng, gp, gb, tg):
    ng[...] = dot(hg[r], wn_ref[...])
    for c0 in range(0, COLS, CHUNK):
        d = ng[c0 : c0 + CHUNK, :] * gain
        normed = nm[r, c0 : c0 + CHUNK, :]
        d_mean = jnp.mean(d, -1, keepdims=True)
        dn_mean = jnp.mean(d * normed, -1, keepdims=True)
        gb16 = (iv[r, c0 : c0 + CHUNK, :] * (d - d_mean - normed * dn_mean)).astype(BF16)
        gb[r, c0 : c0 + CHUNK, :] = gb16
        g = gb16.astype(F32)
        gp[r + 2, PAD + c0 : PAD + c0 + CHUNK, :] = g
        for i in range(3):
            for j in range(3):
                t = g * xp[r + 2 * i, pl.ds(PAD - 2 + 2 * j + c0, CHUNK), :]
                tg[3 * i + j] += t.reshape(CHUNK // 8, 8, CH).sum(0)


def transposed_row(r, cw, gp, cv, dxv, edge):
    for c0 in range(0, COLS, CHUNK):
        acc = cv[r, c0 : c0 + CHUNK, :].astype(F32)
        for i in range(3):
            for j in range(3):
                acc = acc + cw[3 * i + j : 3 * i + j + 1] * gp[r + 4 - 2 * i, pl.ds(PAD + 2 - 2 * j + c0, CHUNK), :]
        dxv[r, c0 : c0 + CHUNK, :] = acc.astype(BF16)
        if c0 == 0:
            edge[0, r] = acc[:16]
        if c0 == COLS - CHUNK:
            edge[1, r] = acc[CHUNK - 16 :]


def kernel(
    act, cot, cw_hbm, gain_hbm, wi_hbm, wo_hbm, scale_hbm, nb_hbm,
    dx, part3,
    cw_ref, gain_ref, scale_ref, nb, av, cv, wi, wo, dxv, xp, gp, wd, wn, sc, nm, iv, hg, ng, gb, og, ig, tg, edge,
    bands, gathered, stage, picked, corner_out, corner_in, halo, ghalo, strips, returned,
    big, small, part1, c2, part2, c3,
    act_s, cot_s, wgt_s, dx_s, own_s,
    seam_s, seam_r, ret_s, ret_r, near_s, near_r, one_s, one_r, three_s, three_r, za_s, za_r,
):
    f, s = lax.axis_index("face"), lax.axis_index("slab")
    x_lo, z, core = s // 16, (s // 2) % DEPTH, s % 2
    a = f * 4 + x_lo * 2 + core
    mirror = SLABS - 1 - s
    up, down = (s + SLABS - 1) % SLABS, (s + 1) % SLABS

    def in_plane(j):
        other = (a + j) % PLANE
        return other, (other // 4, ((other // 2) % 2) * 16 + z * 2 + other % 2)

    def in_depth(j):
        other = (z + j) % DEPTH
        return other, (f, x_lo * 16 + other * 2 + core)

    def loop(low, high, step):
        def body(j, carry):
            step(j)
            return carry

        lax.fori_loop(low, high, body, 0)

    act_in = [pltpu.make_async_copy(act.at[0, r], av.at[r], act_s.at[r]) for r in range(ROWS)]
    cot_in = [pltpu.make_async_copy(cot.at[0, r], cv.at[r], cot_s.at[r]) for r in range(ROWS)]
    wi_in = pltpu.make_async_copy(wi_hbm, wi, wgt_s.at[0])
    wo_in = pltpu.make_async_copy(wo_hbm, wo, wgt_s.at[1])
    little = [(nb_hbm, nb), (cw_hbm, cw_ref), (gain_hbm, gain_ref), (scale_hbm, scale_ref)]
    little_in = [pltpu.make_async_copy(src, dst, wgt_s.at[2 + n]) for n, (src, dst) in enumerate(little)]
    for c in act_in + little_in + [wi_in, wo_in] + cot_in:
        c.start()

    barrier = pltpu.get_barrier_semaphore()

    def greet(device):
        pl.semaphore_signal(barrier, inc=1, device_id=device, device_id_type=MESH)

    loop(0, FACES, lambda j: greet(((f + j) % FACES, mirror)))
    greet((f, up))
    greet((f, down))
    loop(1, PLANE, lambda j: greet(in_plane(j)[1]))
    loop(1, DEPTH, lambda j: greet(in_depth(j)[1]))

    og[...] = jnp.zeros_like(og)
    ig[...] = jnp.zeros_like(ig)
    tg[...] = jnp.zeros_like(tg)
    for r in range(ROWS + 4):
        gp[r, 0:PAD, :] = jnp.zeros((PAD, CH), F32)
        gp[r, PAD + COLS :, :] = jnp.zeros((PAD, CH), F32)
    for c in act_in:
        c.wait()
    for r in range(ROWS):
        left = av[r, 0:16, :].astype(F32)
        right = av[r, COLS - 16 : COLS, :].astype(F32)
        for q in range(2):
            stage[0, q * 8 + r : q * 8 + r + 1, :] = left[q : q + 1]
            stage[1, q * 8 + r : q * 8 + r + 1, :] = right[15 - q : 16 - q]
    bands[...] = stage[...].astype(BF16)
    gathered[0, f] = bands[...]

    def own(r):
        xp[r + 2, PAD : PAD + COLS, :] = av[r].astype(F32)

    loop(0, ROWS, own)

    pl.semaphore_wait(barrier, 2 + FACES + PLANE - 1 + DEPTH - 1)

    def copy(src, dst, send, recv, device):
        return pltpu.make_async_remote_copy(
            src_ref=src, dst_ref=dst, send_sem=send, recv_sem=recv, device_id=device, device_id_type=MESH
        )

    def seam_copy(src, dst, sends, recvs, k, j):
        device = ((f + j) % FACES, mirror if k else s)
        return copy(src, dst.at[k, f], sends.at[k * FACES + j], recvs.at[k * FACES + f], device)

    def seam_start(src, dst, sends, recvs):
        loop(1, FACES, lambda j: seam_copy(src, dst, sends, recvs, 0, j).start())
        loop(0, FACES, lambda j: seam_copy(src, dst, sends, recvs, 1, j).start())

    def seam_wait(src, dst, sends, recvs):
        def arrived(k, j):
            face = (f + j) % FACES
            copy(src, dst.at[k, face], sends.at[k * FACES + j], recvs.at[k * FACES + face], (face, s)).wait_recv()

        loop(1, FACES, lambda j: arrived(0, j))
        loop(0, FACES, lambda j: arrived(1, j))

    def seam_sent(src, dst, sends, recvs):
        loop(1, FACES, lambda j: seam_copy(src, dst, sends, recvs, 0, j).wait_send())
        loop(0, FACES, lambda j: seam_copy(src, dst, sends, recvs, 1, j).wait_send())

    def pick(src):
        out = []
        for e in range(2):
            sf, se, k = nb[0, 0, e, 0], nb[0, 0, e, 2], nb[0, 0, e, 3]
            picked[e] = src[k, sf, se].astype(F32)
            out.append([
                [jnp.where(k == 1, picked[e, q * 8 + 7 - r : q * 8 + 8 - r, :], picked[e, q * 8 + r : q * 8 + r + 1, :]) for r in range(ROWS)]
                for q in range(2)
            ])
        return out

    halo_up = copy(av.at[pl.ds(0, 2)], halo.at[1], near_s.at[0], near_r.at[1], (f, up))
    halo_down = copy(av.at[pl.ds(ROWS - 2, 2)], halo.at[0], near_s.at[1], near_r.at[0], (f, down))
    corner_up = copy(corner_out.at[0], corner_in.at[1], near_s.at[2], near_r.at[3], (f, up))
    corner_down = copy(corner_out.at[1], corner_in.at[0], near_s.at[3], near_r.at[2], (f, down))
    grad_up = copy(gb.at[pl.ds(0, 2)], ghalo.at[1], near_s.at[4], near_r.at[5], (f, up))
    grad_down = copy(gb.at[pl.ds(ROWS - 2, 2)], ghalo.at[0], near_s.at[5], near_r.at[4], (f, down))

    halo_up.start()
    halo_down.start()
    seam_start(bands, gathered, seam_s, seam_r)

    for c in little_in:
        c.wait()
    gain, scale = gain_ref[...], scale_ref[...]
    cw = cw_ref[...]
    wi_in.wait()
    wo_in.wait()
    prepare(wi[...], wo[...], scale, wd, wn)
    for c in cot_in:
        c.wait()

    def cells(pieces, size):
        forward(pieces, size, cw, gain, xp, cv, wi, wd, sc, nm, iv, hg, og, ig)

    def middle(r):
        cells([(r, c0) for c0 in range(64, COLS - 64, 64)], 64)

    def sides(rows):
        cells([(r, c0) for r in rows for c0 in (0, COLS - 64)], 64)

    loop(2, ROWS - 2, middle)

    seam_wait(bands, gathered, seam_s, seam_r)
    strip = pick(gathered)
    for r in range(ROWS):
        for q in range(2):
            xp[r + 2, PAD - 1 - q : PAD - q, :] = strip[0][q][r]
            xp[r + 2, PAD + COLS + q : PAD + COLS + q + 1, :] = strip[1][q][r]
    for e in range(2):
        for q in range(2):
            for t in range(2):
                place = e * 4 + q * 2 + t
                corner_out[0, place : place + 1, :] = strip[e][q][t]
                corner_out[1, place : place + 1, :] = strip[e][q][ROWS - 2 + t]
    corner_up.start()
    corner_down.start()

    sides((2, 3, 4, 5))

    halo_up.wait_recv()
    halo_down.wait_recv()
    inside = (jnp.where(s == 0, 0.0, 1.0), jnp.where(s == SLABS - 1, 0.0, 1.0))
    for side in range(2):
        for t in range(2):
            row = t + side * (ROWS + 2)
            xp[row, PAD : PAD + COLS, :] = halo[side, t].astype(F32) * inside[side]
    loop(0, 4, lambda n: middle(n + n // 2 * 4))

    corner_up.wait_recv()
    corner_down.wait_recv()
    for side in range(2):
        for t in range(2):
            row = t + side * (ROWS + 2)
            for q in range(2):
                left, right = q * 2 + t, 4 + q * 2 + t
                xp[row, PAD - 1 - q : PAD - q, :] = corner_in[side, left : left + 1, :] * inside[side]
                xp[row, PAD + COLS + q : PAD + COLS + q + 1, :] = corner_in[side, right : right + 1, :] * inside[side]

    sides((0, 1, 6, 7))

    products = og[...].T
    out_part = products * (0.5 * FACTOR * scale)
    in_part = ig[...] * FACTOR
    for b in range(HID // SHARE):
        big[b] = out_part[b * SHARE : (b + 1) * SHARE].astype(BF16)
    for b in range(HID // CH):
        for t in range(CH // SHARE):
            big[HID // SHARE + b * (CH // SHARE) + t] = in_part[t * SHARE : (t + 1) * SHARE, b * CH : (b + 1) * CH].astype(BF16)

    def plane_copy(src, dst, sends, recvs, j):
        other, device = in_plane(j)
        return copy(src(other), dst.at[a], sends.at[j], recvs.at[a], device)

    def plane_wait(dst, recvs, j):
        other, device = in_plane(j)
        copy(dst.at[other], dst.at[other], recvs.at[other], recvs.at[other], device).wait_recv()

    def depth_copy(src, dst, sends, recvs, j):
        other, device = in_depth(j)
        return copy(src, dst.at[z], sends.at[j], recvs.at[z], device)

    def depth_wait(dst, recvs, j):
        other, device = in_depth(j)
        copy(dst.at[other], dst.at[other], recvs.at[other], recvs.at[other], device).wait_recv()

    one = partial(plane_copy, lambda other: big.at[other], part1, one_s, one_r)
    two = partial(depth_copy, c2, part2, za_s, za_r)
    three = partial(plane_copy, lambda other: c3, part3, three_s, three_r)

    loop(1, PLANE, lambda j: one(j).start())
    part1[a] = big[a]

    def rows_back(low, high):
        loop(low, high, lambda r: backward(r, gain, xp, wn, nm, iv, hg, ng, gp, gb, tg))

    rows_back(0, 2)
    grad_up.start()
    rows_back(ROWS - 2, ROWS)
    grad_down.start()
    rows_back(2, ROWS - 2)

    small[...] = jnp.zeros_like(small)
    small[0:9, :] = jnp.sum(tg[...], 1) * FACTOR
    in_sum = jnp.sum((ig[...] * wi[...].astype(F32)).T, 0, keepdims=True)
    small[9:10, :] = in_sum / gain * FACTOR
    small[10:11, :] = jnp.sum(og[...].T * wo[...].astype(F32), 0, keepdims=True) * (0.5 * FACTOR)

    loop(1, PLANE, lambda j: plane_wait(part1, one_r, j))
    total = part1[0].astype(F32)
    for b in range(1, PLANE):
        total = total + part1[b].astype(F32)
    c2[:SHARE, :] = total.astype(BF16)
    c2[SHARE:, :] = small[...].astype(BF16)
    part2[z] = c2[...]
    loop(1, DEPTH, lambda j: two(j).start())

    grad_up.wait_recv()
    grad_down.wait_recv()
    for side in range(2):
        for t in range(2):
            gp[t + side * (ROWS + 2), PAD : PAD + COLS, :] = ghalo[side, t].astype(F32) * inside[side]
    for r in range(ROWS):
        left, right = jnp.zeros((8, CH), F32), jnp.zeros((8, CH), F32)
        for i in range(3):
            left = left + cw[3 * i : 3 * i + 1] * gp[r + 4 - 2 * i, PAD : PAD + 8, :]
            right = right + cw[3 * i + 2 : 3 * i + 3] * gp[r + 4 - 2 * i, PAD + COLS - 8 : PAD + COLS, :]
        for q in range(2):
            stage[0, q * 8 + r : q * 8 + r + 1, :] = left[1 - q : 2 - q]
            stage[1, q * 8 + r : q * 8 + r + 1, :] = right[6 + q : 7 + q]
    strips[...] = stage[...].astype(BF16)
    returned[0, f] = strips[...]
    seam_start(strips, returned, ret_s, ret_r)

    def transposed_rows(low, high):
        loop(low, high, lambda r: transposed_row(r, cw, gp, cv, dxv, edge))

    transposed_rows(0, ROWS)

    loop(1, DEPTH, lambda j: depth_wait(part2, za_r, j))
    c3[...] = jnp.sum(part2[...].astype(F32), 0).astype(BF16)
    loop(1, PLANE, lambda j: three(j).start())
    own_share = pltpu.make_async_copy(c3, part3.at[a], own_s.at[0])
    own_share.start()

    seam_wait(strips, returned, ret_s, ret_r)
    back = pick(returned)
    for r in range(ROWS):
        for q in range(2):
            edge[0, r, q : q + 1, :] += back[0][q][r]
            edge[1, r, 15 - q : 16 - q, :] += back[1][q][r]
        dxv[r, 0:16, :] = edge[0, r].astype(BF16)
        dxv[r, COLS - 16 : COLS, :] = edge[1, r].astype(BF16)
    dx_out = [pltpu.make_async_copy(dxv.at[r], dx.at[0, r], dx_s.at[r]) for r in range(ROWS)]
    for c in dx_out:
        c.start()

    seam_sent(bands, gathered, seam_s, seam_r)
    seam_sent(strips, returned, ret_s, ret_r)
    for sent in (halo_up, halo_down, corner_up, corner_down, grad_up, grad_down):
        sent.wait_send()
    loop(1, PLANE, lambda j: one(j).wait_send())
    loop(1, DEPTH, lambda j: two(j).wait_send())
    for c in dx_out:
        c.wait()
    own_share.wait()
    loop(1, PLANE, lambda j: three(j).wait_send())
    loop(1, PLANE, lambda j: plane_wait(part3, three_r, j))


def finish(dx_in, parts, dx, o_conv, o_gain, o_in, o_out, o_scale, sem):
    moved = [pltpu.make_async_copy(dx_in.at[0, r], dx.at[0, r], sem.at[r]) for r in range(ROWS)]
    for c in moved:
        c.start()
    for b in range(HID // SHARE):
        o_out[b * SHARE : (b + 1) * SHARE, :] = parts[b, :SHARE, :].astype(F32)
    for b in range(HID // CH):
        for t in range(CH // SHARE):
            o_in[t * SHARE : (t + 1) * SHARE, b * CH : (b + 1) * CH] = parts[HID // SHARE + b * (CH // SHARE) + t, :SHARE, :].astype(F32)
    sums = parts[0, SHARE:, :].astype(F32)
    for b in range(1, PLANE):
        sums = sums + parts[b, SHARE:, :].astype(F32)
    o_conv[...] = sums[0:9]
    o_gain[...] = sums[9:10]
    o_scale[...] = sums[10:11]
    for c in moved:
        c.wait()


def body(activations, cotangent, conv_weight, norm_gain, w_in, w_out, layer_scale, neighbours):
    vmem = pl.BlockSpec(memory_space=pltpu.VMEM)
    anywhere = pl.BlockSpec(memory_space=pl.ANY)
    dma = pltpu.SemaphoreType.DMA

    def buf(*shape, dtype=F32):
        return pltpu.VMEM(shape, dtype)

    half = partial(buf, dtype=BF16)
    cells = jax.ShapeDtypeStruct((1, ROWS, COLS, CH), BF16)
    dx, parts = pl.pallas_call(
        kernel,
        out_shape=[half(1, ROWS, COLS, CH), half(PLANE, SHARE + 16, CH)],
        in_specs=[anywhere] * 8,
        out_specs=[anywhere, anywhere],
        scratch_shapes=[
            buf(9, CH), buf(1, CH), buf(1, CH), pltpu.SMEM((1, 1, 2, 4), jnp.int32),
            half(ROWS, COLS, CH), half(ROWS, COLS, CH), half(CH, HID), half(HID, CH), half(ROWS, COLS, CH),
            buf(ROWS + 4, WIDE, CH), buf(ROWS + 4, WIDE, CH), half(CH, HID), half(HID, CH),
            half(COLS, CH), buf(ROWS, COLS, CH), buf(ROWS, COLS, CH), half(ROWS, COLS, HID), buf(COLS, CH), half(ROWS, COLS, CH),
            buf(CH, HID), buf(CH, HID), buf(9, 8, CH), buf(2, ROWS, 16, CH),
            half(2, 16, CH), half(2, FACES, 2, 16, CH), buf(2, 16, CH), buf(2, 16, CH), buf(2, 8, CH), buf(2, 8, CH),
            half(2, 2, COLS, CH), half(2, 2, COLS, CH), half(2, 16, CH), half(2, FACES, 2, 16, CH),
            half(PLANE, SHARE, CH), buf(16, CH), half(PLANE, SHARE, CH), half(SHARE + 16, CH),
            half(DEPTH, SHARE + 16, CH), half(SHARE + 16, CH),
            dma((ROWS,)), dma((ROWS,)), dma((6,)), dma((ROWS,)), dma((1,)),
            dma((16,)), dma((16,)), dma((16,)), dma((16,)), dma((6,)), dma((6,)),
            dma((PLANE,)), dma((PLANE,)), dma((PLANE,)), dma((PLANE,)), dma((DEPTH,)), dma((DEPTH,)),
        ],
        compiler_params=pltpu.CompilerParams(collective_id=0, has_side_effects=True, vmem_limit_bytes=48 * 2**20),
    )(*[
        pltpu.with_memory_space_constraint(x, pltpu.HBM)
        for x in (activations, cotangent, conv_weight, norm_gain.reshape(1, CH), w_in, w_out, layer_scale.reshape(1, CH), neighbours)
    ])
    input_gradient, conv_grad, gain_grad, in_grad, out_grad, scale_grad = pl.pallas_call(
        finish,
        out_shape=[
            cells,
            jax.ShapeDtypeStruct((9, CH), F32),
            jax.ShapeDtypeStruct((1, CH), F32),
            jax.ShapeDtypeStruct((CH, HID), F32),
            jax.ShapeDtypeStruct((HID, CH), F32),
            jax.ShapeDtypeStruct((1, CH), F32),
        ],
        in_specs=[anywhere, vmem],
        out_specs=[anywhere] + [vmem] * 5,
        scratch_shapes=[dma((ROWS,))],
        compiler_params=pltpu.CompilerParams(vmem_limit_bytes=8 * 2**20),
    )(dx, parts)
    return input_gradient, conv_grad, gain_grad.reshape(CH), in_grad, out_grad, scale_grad.reshape(CH)


def solution(mesh):
    cells = P("face", "slab", None, None)
    return jax.shard_map(
        body,
        mesh=mesh,
        in_specs=(cells, cells, P(), P(), P(), P(), P(), cells),
        out_specs=(cells, P(), P(), P(), P(), P()),
        check_vma=False,
    )
```

time: 66.1 us -> 51.3 us (0.78)
  Pallas kernels: 59.5 us -> 50.5 us
  local copies, waits for them, and re-layouts: 5.76 us -> 0 us
    pallas_call x1 -> x2, Pallas kernels: 59.5 us -> 50.5 us  [the longest x1 48.7 us: body(): pl.pallas_call(kernel, out_shape=[half(1, ROWS, COLS, CH), half(PLANE, SH...]
    unnamed x16 -> x0, local copies, waits for them, and re-layouts: 5.76 us -> none
where the time goes in v2:
time: 51.3 us; the launch traced here: 51.1 us
  Pallas kernels  50.5 us (98%)
  between operations  0.64 us (1%)
    pallas_call x1, Pallas kernels, body(): pl.pallas_call(kernel, out_shape=[half(1, ROWS, COLS, CH), half(PLANE, SH...  48.7 us
    pallas_call x1, Pallas kernels, body(): pl.pallas_call(finish, out_shape=[cells, jax.ShapeDtypeStruct((9, CH), F3...  1.83 us

profile of v2, /device:TPU:1, one launch (start us, length us, event | category | flops | bytes accessed | tf_op | source)
XLA Modules:
  0.0 51.1 jit_solution(6839817255452136377)
XLA Ops:
  0.6 48.7 %shard_map.127 = (bf16[1,8,512,128]{3,2,1,0:T(8,128)(2,1)S(1)}, bf16[32,48,128]{2,1,0:T(8,128)(2,1)S(1)}) custom-call(bf16[1,8,512,128]{3,2,1,0:T(8,128)(2,1)} %act.1, bf16[1,8,512,128]{3,2,1,0:T(8,128)(2,1)} %cot.1, f32[9,128]{1,0:T(8,128)} %cw_hbm.1, f32[1,128]{1,0:T(1,128)} %bitcast.4, bf16[128,512]{1,0:T(8,128)(2,1)} %wi_hbm.1, bf16[512,128]{1,0:T(8,128)(2,1)} %wo_hbm.1, ...), custom_call_target="tpu_custom_call" | custom-call | tf_op jit(solution)/shard_map/pallas_call | solution.py:416
  49.3 1.8 %shard_map.128 = (bf16[1,8,512,128]{3,2,1,0:T(8,128)(2,1)}, f32[9,128]{1,0:T(8,128)}, f32[1,128]{1,0:T(1,128)}, f32[128,512]{1,0:T(8,128)}, f32[512,128]{1,0:T(8,128)}, /*index=5*/f32[1,128]{1,0:T(1,128)}) custom-call(bf16[1,8,512,128]{3,2,1,0:T(8,128)(2,1)S(1)} %get-tuple-element.14.dx_in, bf16[32,48,128]{2,1,0:T(8,128)(2,1)S(1)} %get-tuple-element.15.parts), custom_call_target="tpu_custom_call" | custom-call | tf_op jit(solution)/shard_map/pallas_call | solution.py:440

commit v3 on v2

--- a/solution.py
+++ b/solution.py
@@ -97,12 +97,12 @@
 
 def kernel(
     act, cot, cw_hbm, gain_hbm, wi_hbm, wo_hbm, scale_hbm, nb_hbm,
-    dx, part3,
+    dx, part3, part5,
     cw_ref, gain_ref, scale_ref, nb, av, cv, wi, wo, dxv, xp, gp, wd, wn, sc, nm, iv, hg, ng, gb, og, ig, tg, edge,
-    bands, gathered, stage, picked, corner_out, corner_in, halo, ghalo, strips, returned,
-    big, small, part1, c2, part2, c3,
+    bands, gathered, stage, picked, corner_out, corner_in, gcorner_out, gcorner_in, halo, ghalo, strips, returned,
+    big, small, small16, smallz, part1, c2, part2, c3, four, part4, five,
     act_s, cot_s, wgt_s, dx_s, own_s,
-    seam_s, seam_r, ret_s, ret_r, near_s, near_r, one_s, one_r, three_s, three_r, za_s, za_r,
+    seam_s, seam_r, ret_s, ret_r, near_s, near_r, one_s, one_r, three_s, three_r, za_s, za_r, zb_s, zb_r, four_s, four_r, five_s, five_r,
 ):
     f, s = lax.axis_index("face"), lax.axis_index("slab")
     x_lo, z, core = s // 16, (s // 2) % DEPTH, s % 2
@@ -205,16 +205,24 @@
             ])
         return out
 
-    halo_up = copy(av.at[pl.ds(0, 2)], halo.at[1], near_s.at[0], near_r.at[1], (f, up))
-    halo_down = copy(av.at[pl.ds(ROWS - 2, 2)], halo.at[0], near_s.at[1], near_r.at[0], (f, down))
-    corner_up = copy(corner_out.at[0], corner_in.at[1], near_s.at[2], near_r.at[3], (f, up))
-    corner_down = copy(corner_out.at[1], corner_in.at[0], near_s.at[3], near_r.at[2], (f, down))
-    grad_up = copy(gb.at[pl.ds(0, 2)], ghalo.at[1], near_s.at[4], near_r.at[5], (f, up))
-    grad_down = copy(gb.at[pl.ds(ROWS - 2, 2)], ghalo.at[0], near_s.at[5], near_r.at[4], (f, down))
-
-    halo_up.start()
-    halo_down.start()
+    def beside(src, dst, n, device):
+        return copy(src, dst, near_s.at[n], near_r.at[n], device)
+
+    halos = [
+        [beside(av.at[ROWS - 2 + t], halo.at[0, t], t, (f, down)) for t in range(2)],
+        [beside(av.at[t], halo.at[1, t], 2 + t, (f, up)) for t in range(2)],
+    ]
+    corners = [beside(corner_out.at[0], corner_in.at[0], 4, (f, down)), beside(corner_out.at[1], corner_in.at[1], 5, (f, up))]
+    grads = [
+        beside(gb.at[pl.ds(ROWS - 2, 2)], ghalo.at[0], 6, (f, down)),
+        beside(gb.at[pl.ds(0, 2)], ghalo.at[1], 7, (f, up)),
+    ]
+    gcorners = [beside(gcorner_out.at[0], gcorner_in.at[0], 8, (f, down)), beside(gcorner_out.at[1], gcorner_in.at[1], 9, (f, up))]
+
     seam_start(bands, gathered, seam_s, seam_r)
+    for t in range(2):
+        for side in range(2):
+            halos[side][t].start()
 
     for c in little_in:
         c.wait()
@@ -235,36 +243,47 @@
     def sides(rows):
         cells([(r, c0) for r in rows for c0 in (0, COLS - 64)], 64)
 
-    loop(2, ROWS - 2, middle)
-
-    seam_wait(bands, gathered, seam_s, seam_r)
-    strip = pick(gathered)
-    for r in range(ROWS):
-        for q in range(2):
-            xp[r + 2, PAD - 1 - q : PAD - q, :] = strip[0][q][r]
-            xp[r + 2, PAD + COLS + q : PAD + COLS + q + 1, :] = strip[1][q][r]
-    for e in range(2):
-        for q in range(2):
-            for t in range(2):
-                place = e * 4 + q * 2 + t
-                corner_out[0, place : place + 1, :] = strip[e][q][t]
-                corner_out[1, place : place + 1, :] = strip[e][q][ROWS - 2 + t]
-    corner_up.start()
-    corner_down.start()
-
+    inside = (jnp.where(s == 0, 0.0, 1.0), jnp.where(s == SLABS - 1, 0.0, 1.0))
+
+    def fill(t):
+        for side in range(2):
+            halos[side][t].wait_recv()
+            xp[t + side * (ROWS + 2), PAD : PAD + COLS, :] = halo[side, t].astype(F32) * inside[side]
+
+    def seam_in():
+        seam_wait(bands, gathered, seam_s, seam_r)
+        strip = pick(gathered)
+        for r in range(ROWS):
+            for q in range(2):
+                xp[r + 2, PAD - 1 - q : PAD - q, :] = strip[0][q][r]
+                xp[r + 2, PAD + COLS + q : PAD + COLS + q + 1, :] = strip[1][q][r]
+        for e in range(2):
+            for q in range(2):
+                for t in range(2):
+                    place = e * 4 + q * 2 + t
+                    corner_out[0, place : place + 1, :] = strip[e][q][ROWS - 2 + t]
+                    corner_out[1, place : place + 1, :] = strip[e][q][t]
+        for c in corners:
+            c.start()
+
+    def in_turn(n):
+        @pl.when(n == 4)
+        def _():
+            fill(0)
+
+        @pl.when(n == 6)
+        def _():
+            seam_in()
+            fill(1)
+
+        late = n // 4
+        middle((1 - late) * (n + 2) + late * (n % 2 * 6 + n // 2 % 2))
+
+    loop(0, ROWS, in_turn)
     sides((2, 3, 4, 5))
 
-    halo_up.wait_recv()
-    halo_down.wait_recv()
-    inside = (jnp.where(s == 0, 0.0, 1.0), jnp.where(s == SLABS - 1, 0.0, 1.0))
-    for side in range(2):
-        for t in range(2):
-            row = t + side * (ROWS + 2)
-            xp[row, PAD : PAD + COLS, :] = halo[side, t].astype(F32) * inside[side]
-    loop(0, 4, lambda n: middle(n + n // 2 * 4))
-
-    corner_up.wait_recv()
-    corner_down.wait_recv()
+    for c in corners:
+        c.wait_recv()
     for side in range(2):
         for t in range(2):
             row = t + side * (ROWS + 2)
@@ -272,7 +291,6 @@
                 left, right = q * 2 + t, 4 + q * 2 + t
                 xp[row, PAD - 1 - q : PAD - q, :] = corner_in[side, left : left + 1, :] * inside[side]
                 xp[row, PAD + COLS + q : PAD + COLS + q + 1, :] = corner_in[side, right : right + 1, :] * inside[side]
-
     sides((0, 1, 6, 7))
 
     products = og[...].T
@@ -303,39 +321,81 @@
     one = partial(plane_copy, lambda other: big.at[other], part1, one_s, one_r)
     two = partial(depth_copy, c2, part2, za_s, za_r)
     three = partial(plane_copy, lambda other: c3, part3, three_s, three_r)
+    small_one = partial(depth_copy, small16, smallz, zb_s, zb_r)
+
+    corner = x_lo * 2 + core
+
+    def quad(j):
+        other = (corner + j) % 4
+        return copy(four, part4.at[corner], four_s.at[j], four_r.at[corner], (f, other // 2 * 16 + z * 2 + other % 2))
+
+    def quad_wait(j):
+        other = (corner + j) % 4
+        copy(four, part4.at[other], four_s.at[j], four_r.at[other], (f, s)).wait_recv()
+
+    def across(j):
+        return copy(five, part5.at[f], five_s.at[j], five_r.at[f], ((f + j) % FACES, s))
+
+    def across_wait(j):
+        other = (f + j) % FACES
+        copy(five, part5.at[other], five_s.at[j], five_r.at[other], (other, s)).wait_recv()
 
     loop(1, PLANE, lambda j: one(j).start())
     part1[a] = big[a]
 
-    def rows_back(low, high):
-        loop(low, high, lambda r: backward(r, gain, xp, wn, nm, iv, hg, ng, gp, gb, tg))
-
-    rows_back(0, 2)
-    grad_up.start()
-    rows_back(ROWS - 2, ROWS)
-    grad_down.start()
-    rows_back(2, ROWS - 2)
+    def send_grads(side):
+        first = 0 if side else ROWS - 2
+        for t in range(2):
+            left = gp[first + t + 2, PAD : PAD + 8, :]
+            right = gp[first + t + 2, PAD + COLS - 8 : PAD + COLS, :]
+            for c in range(2):
+                gcorner_out[side, c * 2 + t : c * 2 + t + 1, :] = left[c : c + 1]
+                gcorner_out[side, 4 + c * 2 + t : 5 + c * 2 + t, :] = right[6 + c : 7 + c]
+        gcorners[side].start()
+        grads[side].start()
+
+    def back_in_turn(n):
+        late = n // 4
+        backward((1 - late) * (n % 2 + n // 2 * 6) + late * (n - 2), gain, xp, wn, nm, iv, hg, ng, gp, gb, tg)
+
+        @pl.when(n == 1)
+        def _():
+            send_grads(1)
+
+        @pl.when(n == 3)
+        def _():
+            send_grads(0)
+
+    loop(0, 6, back_in_turn)
+
+    loop(1, PLANE, lambda j: plane_wait(part1, one_r, j))
+    total = part1[0].astype(F32)
+    for b in range(1, PLANE):
+        total = total + part1[b].astype(F32)
+    c2[...] = total.astype(BF16)
+    part2[z] = c2[...]
+    loop(1, DEPTH, lambda j: two(j).start())
+
+    loop(6, ROWS, back_in_turn)
 
     small[...] = jnp.zeros_like(small)
     small[0:9, :] = jnp.sum(tg[...], 1) * FACTOR
     in_sum = jnp.sum((ig[...] * wi[...].astype(F32)).T, 0, keepdims=True)
     small[9:10, :] = in_sum / gain * FACTOR
     small[10:11, :] = jnp.sum(og[...].T * wo[...].astype(F32), 0, keepdims=True) * (0.5 * FACTOR)
-
-    loop(1, PLANE, lambda j: plane_wait(part1, one_r, j))
-    total = part1[0].astype(F32)
-    for b in range(1, PLANE):
-        total = total + part1[b].astype(F32)
-    c2[:SHARE, :] = total.astype(BF16)
-    c2[SHARE:, :] = small[...].astype(BF16)
-    part2[z] = c2[...]
-    loop(1, DEPTH, lambda j: two(j).start())
-
-    grad_up.wait_recv()
-    grad_down.wait_recv()
+    small16[...] = small[...].astype(BF16)
+    smallz[z] = small16[...]
+    loop(1, DEPTH, lambda j: small_one(j).start())
+
+    for c in gcorners:
+        c.wait_recv()
     for side in range(2):
         for t in range(2):
-            gp[t + side * (ROWS + 2), PAD : PAD + COLS, :] = ghalo[side, t].astype(F32) * inside[side]
+            row = t + side * (ROWS + 2)
+            for c in range(2):
+                left, right = c * 2 + t, 4 + c * 2 + t
+                gp[row, PAD + c : PAD + c + 1, :] = gcorner_in[side, left : left + 1, :] * inside[side]
+                gp[row, PAD + COLS - 2 + c : PAD + COLS - 1 + c, :] = gcorner_in[side, right : right + 1, :] * inside[side]
     for r in range(ROWS):
         left, right = jnp.zeros((8, CH), F32), jnp.zeros((8, CH), F32)
         for i in range(3):
@@ -348,16 +408,32 @@
     returned[0, f] = strips[...]
     seam_start(strips, returned, ret_s, ret_r)
 
-    def transposed_rows(low, high):
-        loop(low, high, lambda r: transposed_row(r, cw, gp, cv, dxv, edge))
-
-    transposed_rows(0, ROWS)
-
     loop(1, DEPTH, lambda j: depth_wait(part2, za_r, j))
     c3[...] = jnp.sum(part2[...].astype(F32), 0).astype(BF16)
     loop(1, PLANE, lambda j: three(j).start())
     own_share = pltpu.make_async_copy(c3, part3.at[a], own_s.at[0])
     own_share.start()
+    loop(1, DEPTH, lambda j: depth_wait(smallz, zb_r, j))
+    four[...] = jnp.sum(smallz[...].astype(F32), 0).astype(BF16)
+    part4[corner] = four[...]
+    loop(1, 4, lambda j: quad(j).start())
+
+    for side in range(2):
+        grads[side].wait_recv()
+        for t in range(2):
+            gp[t + side * (ROWS + 2), PAD : PAD + COLS, :] = ghalo[side, t].astype(F32) * inside[side]
+
+    def transposed_rows(low, high):
+        loop(low, high, lambda r: transposed_row(r, cw, gp, cv, dxv, edge))
+
+    transposed_rows(0, 4)
+
+    loop(1, 4, quad_wait)
+    five[...] = jnp.sum(part4[...].astype(F32), 0).astype(BF16)
+    loop(1, FACES, lambda j: across(j).start())
+    own_small = pltpu.make_async_copy(five, part5.at[f], own_s.at[1])
+    own_small.start()
+    transposed_rows(4, ROWS)
 
     seam_wait(strips, returned, ret_s, ret_r)
     back = pick(returned)
@@ -373,29 +449,32 @@
 
     seam_sent(bands, gathered, seam_s, seam_r)
     seam_sent(strips, returned, ret_s, ret_r)
-    for sent in (halo_up, halo_down, corner_up, corner_down, grad_up, grad_down):
+    for sent in halos[0] + halos[1] + corners + grads + gcorners:
         sent.wait_send()
     loop(1, PLANE, lambda j: one(j).wait_send())
     loop(1, DEPTH, lambda j: two(j).wait_send())
+    loop(1, DEPTH, lambda j: small_one(j).wait_send())
     for c in dx_out:
         c.wait()
     own_share.wait()
+    own_small.wait()
+    loop(1, 4, lambda j: quad(j).wait_send())
     loop(1, PLANE, lambda j: three(j).wait_send())
+    loop(1, FACES, lambda j: across(j).wait_send())
     loop(1, PLANE, lambda j: plane_wait(part3, three_r, j))
-
-
-def finish(dx_in, parts, dx, o_conv, o_gain, o_in, o_out, o_scale, sem):
+    loop(1, FACES, across_wait)
+
+
+def finish(dx_in, parts, smalls, dx, o_conv, o_gain, o_in, o_out, o_scale, sem):
     moved = [pltpu.make_async_copy(dx_in.at[0, r], dx.at[0, r], sem.at[r]) for r in range(ROWS)]
     for c in moved:
         c.start()
     for b in range(HID // SHARE):
-        o_out[b * SHARE : (b + 1) * SHARE, :] = parts[b, :SHARE, :].astype(F32)
+        o_out[b * SHARE : (b + 1) * SHARE, :] = parts[b].astype(F32)
     for b in range(HID // CH):
         for t in range(CH // SHARE):
-            o_in[t * SHARE : (t + 1) * SHARE, b * CH : (b + 1) * CH] = parts[HID // SHARE + b * (CH // SHARE) + t, :SHARE, :].astype(F32)
-    sums = parts[0, SHARE:, :].astype(F32)
-    for b in range(1, PLANE):
-        sums = sums + parts[b, SHARE:, :].astype(F32)
+            o_in[t * SHARE : (t + 1) * SHARE, b * CH : (b + 1) * CH] = parts[HID // SHARE + b * (CH // SHARE) + t].astype(F32)
+    sums = jnp.sum(smalls[...].astype(F32), 0)
     o_conv[...] = sums[0:9]
     o_gain[...] = sums[9:10]
     o_scale[...] = sums[10:11]
@@ -413,24 +492,26 @@
 
     half = partial(buf, dtype=BF16)
     cells = jax.ShapeDtypeStruct((1, ROWS, COLS, CH), BF16)
-    dx, parts = pl.pallas_call(
+    dx, parts, smalls = pl.pallas_call(
         kernel,
-        out_shape=[half(1, ROWS, COLS, CH), half(PLANE, SHARE + 16, CH)],
+        out_shape=[half(1, ROWS, COLS, CH), half(PLANE, SHARE, CH), half(FACES, 16, CH)],
         in_specs=[anywhere] * 8,
-        out_specs=[anywhere, anywhere],
+        out_specs=[anywhere] * 3,
         scratch_shapes=[
             buf(9, CH), buf(1, CH), buf(1, CH), pltpu.SMEM((1, 1, 2, 4), jnp.int32),
             half(ROWS, COLS, CH), half(ROWS, COLS, CH), half(CH, HID), half(HID, CH), half(ROWS, COLS, CH),
             buf(ROWS + 4, WIDE, CH), buf(ROWS + 4, WIDE, CH), half(CH, HID), half(HID, CH),
             half(COLS, CH), buf(ROWS, COLS, CH), buf(ROWS, COLS, CH), half(ROWS, COLS, HID), buf(COLS, CH), half(ROWS, COLS, CH),
             buf(CH, HID), buf(CH, HID), buf(9, 8, CH), buf(2, ROWS, 16, CH),
-            half(2, 16, CH), half(2, FACES, 2, 16, CH), buf(2, 16, CH), buf(2, 16, CH), buf(2, 8, CH), buf(2, 8, CH),
+            half(2, 16, CH), half(2, FACES, 2, 16, CH), buf(2, 16, CH), buf(2, 16, CH), buf(2, 8, CH), buf(2, 8, CH), buf(2, 8, CH), buf(2, 8, CH),
             half(2, 2, COLS, CH), half(2, 2, COLS, CH), half(2, 16, CH), half(2, FACES, 2, 16, CH),
-            half(PLANE, SHARE, CH), buf(16, CH), half(PLANE, SHARE, CH), half(SHARE + 16, CH),
-            half(DEPTH, SHARE + 16, CH), half(SHARE + 16, CH),
-            dma((ROWS,)), dma((ROWS,)), dma((6,)), dma((ROWS,)), dma((1,)),
-            dma((16,)), dma((16,)), dma((16,)), dma((16,)), dma((6,)), dma((6,)),
-            dma((PLANE,)), dma((PLANE,)), dma((PLANE,)), dma((PLANE,)), dma((DEPTH,)), dma((DEPTH,)),
+            half(PLANE, SHARE, CH), buf(16, CH), half(16, CH), half(DEPTH, 16, CH), half(PLANE, SHARE, CH), half(SHARE, CH),
+            half(DEPTH, SHARE, CH), half(SHARE, CH), half(16, CH), half(4, 16, CH), half(16, CH),
+            dma((ROWS,)), dma((ROWS,)), dma((6,)), dma((ROWS,)), dma((2,)),
+            dma((16,)), dma((16,)), dma((16,)), dma((16,)), dma((10,)), dma((10,)),
+            dma((PLANE,)), dma((PLANE,)), dma((PLANE,)), dma((PLANE,)),
+            dma((DEPTH,)), dma((DEPTH,)), dma((DEPTH,)), dma((DEPTH,)),
+            dma((4,)), dma((4,)), dma((FACES,)), dma((FACES,)),
         ],
         compiler_params=pltpu.CompilerParams(collective_id=0, has_side_effects=True, vmem_limit_bytes=48 * 2**20),
     )(*[
@@ -447,11 +528,11 @@
             jax.ShapeDtypeStruct((HID, CH), F32),
             jax.ShapeDtypeStruct((1, CH), F32),
         ],
-        in_specs=[anywhere, vmem],
+        in_specs=[anywhere, vmem, vmem],
         out_specs=[anywhere] + [vmem] * 5,
         scratch_shapes=[dma((ROWS,))],
         compiler_params=pltpu.CompilerParams(vmem_limit_bytes=8 * 2**20),
-    )(dx, parts)
+    )(dx, parts, smalls)
     return input_gradient, conv_grad, gain_grad.reshape(CH), in_grad, out_grad, scale_grad.reshape(CH)
 
 

time: 51.3 us -> 49.8 us (0.971)
  Pallas kernels: 50.5 us -> 49.1 us
    pallas_call x1, Pallas kernels: 48.7 us -> 47.3 us  [body(): pl.pallas_call(kernel, out_shape=[half(1, ROWS, COLS, CH), half(PLANE, SH...]
where the time goes in v3:
time: 49.8 us; the launch traced here: 49.7 us
  Pallas kernels  49.1 us (99%)
  between operations  0.64 us (1%)
    pallas_call x1, Pallas kernels, body(): pl.pallas_call(kernel, out_shape=[half(1, ROWS, COLS, CH), half(PLANE, SH...  47.3 us
    pallas_call x1, Pallas kernels, body(): pl.pallas_call(finish, out_shape=[cells, jax.ShapeDtypeStruct((9, CH), F3...  1.83 us

profile of v3, /device:TPU:1, one launch (start us, length us, event | category | flops | bytes accessed | tf_op | source)
XLA Modules:
  0.0 49.7 jit_solution(10215356288543125310)
XLA Ops:
  0.6 47.3 %shard_map.127 = (bf16[1,8,512,128]{3,2,1,0:T(8,128)(2,1)S(1)}, bf16[32,32,128]{2,1,0:T(8,128)(2,1)S(1)}, bf16[8,16,128]{2,1,0:T(8,128)(2,1)S(1)}) custom-call(bf16[1,8,512,128]{3,2,1,0:T(8,128)(2,1)} %act.1, bf16[1,8,512,128]{3,2,1,0:T(8,128)(2,1)} %cot.1, f32[9,128]{1,0:T(8,128)} %cw_hbm.1, f32[1,128]{1,0:T(1,128)} %bitcast.4, bf16[128,512]{1,0:T(8,128)(2,1)} %wi_hbm.1, ...), custom_call_target="tpu_custom_call" | custom-call | tf_op jit(solution)/shard_map/pallas_call | solution.py:495
  47.9 1.8 %shard_map.128 = (bf16[1,8,512,128]{3,2,1,0:T(8,128)(2,1)}, f32[9,128]{1,0:T(8,128)}, f32[1,128]{1,0:T(1,128)}, f32[128,512]{1,0:T(8,128)}, f32[512,128]{1,0:T(8,128)}, /*index=5*/f32[1,128]{1,0:T(1,128)}) custom-call(bf16[1,8,512,128]{3,2,1,0:T(8,128)(2,1)S(1)} %get-tuple-element.15.dx_in, bf16[32,32,128]{2,1,0:T(8,128)(2,1)S(1)} %get-tuple-element.16.parts, ...), custom_call_target="tpu_custom_call" | custom-call | tf_op jit(solution)/shard_map/pallas_call | solution.py:521

commit v4 on v3

--- a/solution.py
+++ b/solution.py
@@ -98,7 +98,7 @@
 def kernel(
     act, cot, cw_hbm, gain_hbm, wi_hbm, wo_hbm, scale_hbm, nb_hbm,
     dx, part3, part5,
-    cw_ref, gain_ref, scale_ref, nb, av, cv, wi, wo, dxv, xp, gp, wd, wn, sc, nm, iv, hg, ng, gb, og, ig, tg, edge,
+    cw_ref, gain_ref, scale_ref, nb, av, cv, wi, wo, dxv, xp, gp, wd, wn, sc, nm, iv, hg, ng, gb, og, ig, tg, edge, edge16,
     bands, gathered, stage, picked, corner_out, corner_in, gcorner_out, gcorner_in, halo, ghalo, strips, returned,
     big, small, small16, smallz, part1, c2, part2, c3, four, part4, five,
     act_s, cot_s, wgt_s, dx_s, own_s,
@@ -219,10 +219,11 @@
     ]
     gcorners = [beside(gcorner_out.at[0], gcorner_in.at[0], 8, (f, down)), beside(gcorner_out.at[1], gcorner_in.at[1], 9, (f, up))]
 
+    for side in range(2):
+        halos[side][0].start()
     seam_start(bands, gathered, seam_s, seam_r)
-    for t in range(2):
-        for side in range(2):
-            halos[side][t].start()
+    for side in range(2):
+        halos[side][1].start()
 
     for c in little_in:
         c.wait()
@@ -274,13 +275,13 @@
         @pl.when(n == 6)
         def _():
             seam_in()
+            sides((2, 3, 4, 5))
             fill(1)
 
         late = n // 4
         middle((1 - late) * (n + 2) + late * (n % 2 * 6 + n // 2 % 2))
 
     loop(0, ROWS, in_turn)
-    sides((2, 3, 4, 5))
 
     for c in corners:
         c.wait_recv()
@@ -321,17 +322,17 @@
     one = partial(plane_copy, lambda other: big.at[other], part1, one_s, one_r)
     two = partial(depth_copy, c2, part2, za_s, za_r)
     three = partial(plane_copy, lambda other: c3, part3, three_s, three_r)
-    small_one = partial(depth_copy, small16, smallz, zb_s, zb_r)
+    small_one = partial(depth_copy, four, smallz, zb_s, zb_r)
 
     corner = x_lo * 2 + core
 
     def quad(j):
         other = (corner + j) % 4
-        return copy(four, part4.at[corner], four_s.at[j], four_r.at[corner], (f, other // 2 * 16 + z * 2 + other % 2))
+        return copy(small16, part4.at[corner], four_s.at[j], four_r.at[corner], (f, other // 2 * 16 + z * 2 + other % 2))
 
     def quad_wait(j):
         other = (corner + j) % 4
-        copy(four, part4.at[other], four_s.at[j], four_r.at[other], (f, s)).wait_recv()
+        copy(small16, part4.at[other], four_s.at[j], four_r.at[other], (f, s)).wait_recv()
 
     def across(j):
         return copy(five, part5.at[f], five_s.at[j], five_r.at[f], ((f + j) % FACES, s))
@@ -384,8 +385,8 @@
     small[9:10, :] = in_sum / gain * FACTOR
     small[10:11, :] = jnp.sum(og[...].T * wo[...].astype(F32), 0, keepdims=True) * (0.5 * FACTOR)
     small16[...] = small[...].astype(BF16)
-    smallz[z] = small16[...]
-    loop(1, DEPTH, lambda j: small_one(j).start())
+    part4[corner] = small16[...]
+    loop(1, 4, lambda j: quad(j).start())
 
     for c in gcorners:
         c.wait_recv()
@@ -408,32 +409,38 @@
     returned[0, f] = strips[...]
     seam_start(strips, returned, ret_s, ret_r)
 
+    def dx_copy(r):
+        inner = pl.ds(16, COLS - 32)
+        return pltpu.make_async_copy(dxv.at[r, inner], dx.at[0, r, inner], dx_s.at[r])
+
+    def transposed(r):
+        transposed_row(r, cw, gp, cv, dxv, edge)
+        dx_copy(r).start()
+
+    loop(2, ROWS - 2, transposed)
+
+    loop(1, 4, quad_wait)
+    four[...] = jnp.sum(part4[...].astype(F32), 0).astype(BF16)
+    smallz[z] = four[...]
+    loop(1, DEPTH, lambda j: small_one(j).start())
+
     loop(1, DEPTH, lambda j: depth_wait(part2, za_r, j))
     c3[...] = jnp.sum(part2[...].astype(F32), 0).astype(BF16)
     loop(1, PLANE, lambda j: three(j).start())
     own_share = pltpu.make_async_copy(c3, part3.at[a], own_s.at[0])
     own_share.start()
     loop(1, DEPTH, lambda j: depth_wait(smallz, zb_r, j))
-    four[...] = jnp.sum(smallz[...].astype(F32), 0).astype(BF16)
-    part4[corner] = four[...]
-    loop(1, 4, lambda j: quad(j).start())
+    five[...] = jnp.sum(smallz[...].astype(F32), 0).astype(BF16)
+    loop(1, FACES, lambda j: across(j).start())
+    own_small = pltpu.make_async_copy(five, part5.at[f], own_s.at[1])
+    own_small.start()
 
     for side in range(2):
         grads[side].wait_recv()
         for t in range(2):
             gp[t + side * (ROWS + 2), PAD : PAD + COLS, :] = ghalo[side, t].astype(F32) * inside[side]
 
-    def transposed_rows(low, high):
-        loop(low, high, lambda r: transposed_row(r, cw, gp, cv, dxv, edge))
-
-    transposed_rows(0, 4)
-
-    loop(1, 4, quad_wait)
-    five[...] = jnp.sum(part4[...].astype(F32), 0).astype(BF16)
-    loop(1, FACES, lambda j: across(j).start())
-    own_small = pltpu.make_async_copy(five, part5.at[f], own_s.at[1])
-    own_small.start()
-    transposed_rows(4, ROWS)
+    loop(0, 4, lambda n: transposed(n % 2 + n // 2 * 6))
 
     seam_wait(strips, returned, ret_s, ret_r)
     back = pick(returned)
@@ -441,10 +448,11 @@
         for q in range(2):
             edge[0, r, q : q + 1, :] += back[0][q][r]
             edge[1, r, 15 - q : 16 - q, :] += back[1][q][r]
-        dxv[r, 0:16, :] = edge[0, r].astype(BF16)
-        dxv[r, COLS - 16 : COLS, :] = edge[1, r].astype(BF16)
-    dx_out = [pltpu.make_async_copy(dxv.at[r], dx.at[0, r], dx_s.at[r]) for r in range(ROWS)]
-    for c in dx_out:
+    edge16[...] = edge[...].astype(BF16)
+    edge_out = [
+        pltpu.make_async_copy(edge16.at[e], dx.at[0, :, pl.ds(e * (COLS - 16), 16)], dx_s.at[ROWS + e]) for e in range(2)
+    ]
+    for c in edge_out:
         c.start()
 
     seam_sent(bands, gathered, seam_s, seam_r)
@@ -454,7 +462,8 @@
     loop(1, PLANE, lambda j: one(j).wait_send())
     loop(1, DEPTH, lambda j: two(j).wait_send())
     loop(1, DEPTH, lambda j: small_one(j).wait_send())
-    for c in dx_out:
+    loop(0, ROWS, lambda r: dx_copy(r).wait())
+    for c in edge_out:
         c.wait()
     own_share.wait()
     own_small.wait()
@@ -502,12 +511,12 @@
             half(ROWS, COLS, CH), half(ROWS, COLS, CH), half(CH, HID), half(HID, CH), half(ROWS, COLS, CH),
             buf(ROWS + 4, WIDE, CH), buf(ROWS + 4, WIDE, CH), half(CH, HID), half(HID, CH),
             half(COLS, CH), buf(ROWS, COLS, CH), buf(ROWS, COLS, CH), half(ROWS, COLS, HID), buf(COLS, CH), half(ROWS, COLS, CH),
-            buf(CH, HID), buf(CH, HID), buf(9, 8, CH), buf(2, ROWS, 16, CH),
+            buf(CH, HID), buf(CH, HID), buf(9, 8, CH), buf(2, ROWS, 16, CH), half(2, ROWS, 16, CH),
             half(2, 16, CH), half(2, FACES, 2, 16, CH), buf(2, 16, CH), buf(2, 16, CH), buf(2, 8, CH), buf(2, 8, CH), buf(2, 8, CH), buf(2, 8, CH),
             half(2, 2, COLS, CH), half(2, 2, COLS, CH), half(2, 16, CH), half(2, FACES, 2, 16, CH),
             half(PLANE, SHARE, CH), buf(16, CH), half(16, CH), half(DEPTH, 16, CH), half(PLANE, SHARE, CH), half(SHARE, CH),
             half(DEPTH, SHARE, CH), half(SHARE, CH), half(16, CH), half(4, 16, CH), half(16, CH),
-            dma((ROWS,)), dma((ROWS,)), dma((6,)), dma((ROWS,)), dma((2,)),
+            dma((ROWS,)), dma((ROWS,)), dma((6,)), dma((ROWS + 2,)), dma((2,)),
             dma((16,)), dma((16,)), dma((16,)), dma((16,)), dma((10,)), dma((10,)),
             dma((PLANE,)), dma((PLANE,)), dma((PLANE,)), dma((PLANE,)),
             dma((DEPTH,)), dma((DEPTH,)), dma((DEPTH,)), dma((DEPTH,)),

time: 49.8 us -> 48.5 us (0.974)
  Pallas kernels: 49.1 us -> 47.8 us
    pallas_call x1, Pallas kernels: 47.3 us -> 45.9 us  [body(): pl.pallas_call(kernel, out_shape=[half(1, ROWS, COLS, CH), half(PLANE, SH...]
where the time goes in v4:
time: 48.5 us; the launch traced here: 48.4 us
  Pallas kernels  47.8 us (99%)
  between operations  0.64 us (1%)
    pallas_call x1, Pallas kernels, body(): pl.pallas_call(kernel, out_shape=[half(1, ROWS, COLS, CH), half(PLANE, SH...  45.9 us
    pallas_call x1, Pallas kernels, body(): pl.pallas_call(finish, out_shape=[cells, jax.ShapeDtypeStruct((9, CH), F3...  1.83 us

profile of v4, /device:TPU:1, one launch (start us, length us, event | category | flops | bytes accessed | tf_op | source)
XLA Modules:
  0.0 48.4 jit_solution(6659562477071324470)
XLA Ops:
  0.6 45.9 %shard_map.127 = (bf16[1,8,512,128]{3,2,1,0:T(8,128)(2,1)S(1)}, bf16[32,32,128]{2,1,0:T(8,128)(2,1)S(1)}, bf16[8,16,128]{2,1,0:T(8,128)(2,1)S(1)}) custom-call(bf16[1,8,512,128]{3,2,1,0:T(8,128)(2,1)} %act.1, bf16[1,8,512,128]{3,2,1,0:T(8,128)(2,1)} %cot.1, f32[9,128]{1,0:T(8,128)} %cw_hbm.1, f32[1,128]{1,0:T(1,128)} %bitcast.4, bf16[128,512]{1,0:T(8,128)(2,1)} %wi_hbm.1, ...), custom_call_target="tpu_custom_call" | custom-call | tf_op jit(solution)/shard_map/pallas_call | solution.py:504
  46.6 1.8 %shard_map.128 = (bf16[1,8,512,128]{3,2,1,0:T(8,128)(2,1)}, f32[9,128]{1,0:T(8,128)}, f32[1,128]{1,0:T(1,128)}, f32[128,512]{1,0:T(8,128)}, f32[512,128]{1,0:T(8,128)}, /*index=5*/f32[1,128]{1,0:T(1,128)}) custom-call(bf16[1,8,512,128]{3,2,1,0:T(8,128)(2,1)S(1)} %get-tuple-element.15.dx_in, bf16[32,32,128]{2,1,0:T(8,128)(2,1)S(1)} %get-tuple-element.16.parts, ...), custom_call_target="tpu_custom_call" | custom-call | tf_op jit(solution)/shard_map/pallas_call | solution.py:530

commit v5 on v4

--- a/solution.py
+++ b/solution.py
@@ -367,17 +367,7 @@
         def _():
             send_grads(0)
 
-    loop(0, 6, back_in_turn)
-
-    loop(1, PLANE, lambda j: plane_wait(part1, one_r, j))
-    total = part1[0].astype(F32)
-    for b in range(1, PLANE):
-        total = total + part1[b].astype(F32)
-    c2[...] = total.astype(BF16)
-    part2[z] = c2[...]
-    loop(1, DEPTH, lambda j: two(j).start())
-
-    loop(6, ROWS, back_in_turn)
+    loop(0, ROWS, back_in_turn)
 
     small[...] = jnp.zeros_like(small)
     small[0:9, :] = jnp.sum(tg[...], 1) * FACTOR
@@ -387,6 +377,19 @@
     small16[...] = small[...].astype(BF16)
     part4[corner] = small16[...]
     loop(1, 4, lambda j: quad(j).start())
+
+    loop(1, PLANE, lambda j: plane_wait(part1, one_r, j))
+    total = part1[0].astype(F32)
+    for b in range(1, PLANE):
+        total = total + part1[b].astype(F32)
+    c2[...] = total.astype(BF16)
+    part2[z] = c2[...]
+    loop(1, DEPTH, lambda j: two(j).start())
+
+    loop(1, 4, quad_wait)
+    four[...] = jnp.sum(part4[...].astype(F32), 0).astype(BF16)
+    smallz[z] = four[...]
+    loop(1, DEPTH, lambda j: small_one(j).start())
 
     for c in gcorners:
         c.wait_recv()
@@ -418,11 +421,6 @@
         dx_copy(r).start()
 
     loop(2, ROWS - 2, transposed)
-
-    loop(1, 4, quad_wait)
-    four[...] = jnp.sum(part4[...].astype(F32), 0).astype(BF16)
-    smallz[z] = four[...]
-    loop(1, DEPTH, lambda j: small_one(j).start())
 
     loop(1, DEPTH, lambda j: depth_wait(part2, za_r, j))
     c3[...] = jnp.sum(part2[...].astype(F32), 0).astype(BF16)

time: 48.5 us -> 48.1 us (level)
  Pallas kernels: 47.8 us -> 47.3 us
where the time goes in v5:
time: 48.1 us; the launch traced here: 48 us
  Pallas kernels  47.3 us (98%)
  between operations  0.64 us (1%)
    pallas_call x1, Pallas kernels, body(): pl.pallas_call(kernel, out_shape=[half(1, ROWS, COLS, CH), half(PLANE, SH...  45.5 us
    pallas_call x1, Pallas kernels, body(): pl.pallas_call(finish, out_shape=[cells, jax.ShapeDtypeStruct((9, CH), F3...  1.83 us

profile of v5, /device:TPU:1, one launch (start us, length us, event | category | flops | bytes accessed | tf_op | source)
XLA Modules:
  0.0 48.0 jit_solution(3822548747655340817)
XLA Ops:
  0.6 45.5 %shard_map.127 = (bf16[1,8,512,128]{3,2,1,0:T(8,128)(2,1)S(1)}, bf16[32,32,128]{2,1,0:T(8,128)(2,1)S(1)}, bf16[8,16,128]{2,1,0:T(8,128)(2,1)S(1)}) custom-call(bf16[1,8,512,128]{3,2,1,0:T(8,128)(2,1)} %act.1, bf16[1,8,512,128]{3,2,1,0:T(8,128)(2,1)} %cot.1, f32[9,128]{1,0:T(8,128)} %cw_hbm.1, f32[1,128]{1,0:T(1,128)} %bitcast.4, bf16[128,512]{1,0:T(8,128)(2,1)} %wi_hbm.1, ...), custom_call_target="tpu_custom_call" | custom-call | tf_op jit(solution)/shard_map/pallas_call | solution.py:502
  46.1 1.8 %shard_map.128 = (bf16[1,8,512,128]{3,2,1,0:T(8,128)(2,1)}, f32[9,128]{1,0:T(8,128)}, f32[1,128]{1,0:T(1,128)}, f32[128,512]{1,0:T(8,128)}, f32[512,128]{1,0:T(8,128)}, /*index=5*/f32[1,128]{1,0:T(1,128)}) custom-call(bf16[1,8,512,128]{3,2,1,0:T(8,128)(2,1)S(1)} %get-tuple-element.15.dx_in, bf16[32,32,128]{2,1,0:T(8,128)(2,1)S(1)} %get-tuple-element.16.parts, ...), custom_call_target="tpu_custom_call" | custom-call | tf_op jit(solution)/shard_map/pallas_call | solution.py:528

commit v6 on v5

--- a/solution.py
+++ b/solution.py
@@ -219,9 +219,9 @@
     ]
     gcorners = [beside(gcorner_out.at[0], gcorner_in.at[0], 8, (f, down)), beside(gcorner_out.at[1], gcorner_in.at[1], 9, (f, up))]
 
+    seam_start(bands, gathered, seam_s, seam_r)
     for side in range(2):
         halos[side][0].start()
-    seam_start(bands, gathered, seam_s, seam_r)
     for side in range(2):
         halos[side][1].start()
 

time: 48.1 us -> 47.9 us (level)
  no operation moved by 1% of the time
where the time goes in v6:
time: 47.9 us; the launch traced here: 47.8 us
  Pallas kernels  47.2 us (99%)
  between operations  0.64 us (1%)
    pallas_call x1, Pallas kernels, body(): pl.pallas_call(kernel, out_shape=[half(1, ROWS, COLS, CH), half(PLANE, SH...  45.3 us
    pallas_call x1, Pallas kernels, body(): pl.pallas_call(finish, out_shape=[cells, jax.ShapeDtypeStruct((9, CH), F3...  1.83 us

profile of v6, /device:TPU:1, one launch (start us, length us, event | category | flops | bytes accessed | tf_op | source)
XLA Modules:
  0.0 47.8 jit_solution(18204844646811903100)
XLA Ops:
  0.6 45.3 %shard_map.127 = (bf16[1,8,512,128]{3,2,1,0:T(8,128)(2,1)S(1)}, bf16[32,32,128]{2,1,0:T(8,128)(2,1)S(1)}, bf16[8,16,128]{2,1,0:T(8,128)(2,1)S(1)}) custom-call(bf16[1,8,512,128]{3,2,1,0:T(8,128)(2,1)} %act.1, bf16[1,8,512,128]{3,2,1,0:T(8,128)(2,1)} %cot.1, f32[9,128]{1,0:T(8,128)} %cw_hbm.1, f32[1,128]{1,0:T(1,128)} %bitcast.4, bf16[128,512]{1,0:T(8,128)(2,1)} %wi_hbm.1, ...), custom_call_target="tpu_custom_call" | custom-call | tf_op jit(solution)/shard_map/pallas_call | solution.py:502
  46.0 1.8 %shard_map.128 = (bf16[1,8,512,128]{3,2,1,0:T(8,128)(2,1)}, f32[9,128]{1,0:T(8,128)}, f32[1,128]{1,0:T(1,128)}, f32[128,512]{1,0:T(8,128)}, f32[512,128]{1,0:T(8,128)}, /*index=5*/f32[1,128]{1,0:T(1,128)}) custom-call(bf16[1,8,512,128]{3,2,1,0:T(8,128)(2,1)S(1)} %get-tuple-element.15.dx_in, bf16[32,32,128]{2,1,0:T(8,128)(2,1)S(1)} %get-tuple-element.16.parts, ...), custom_call_target="tpu_custom_call" | custom-call | tf_op jit(solution)/shard_map/pallas_call | solution.py:528
